TPU v7x, 128 devices: a whole 4x4x4 slice. The times are simulated.
128 devices in a mesh: section: 2 (over x_lo), tensor: 16 (over x_hi, z, core), dp: 4 (over y).
Axes of the slice: x: 4 (x_hi: 2, x_lo: 2; x = x_hi * 2 + x_lo), y: 4, z: 4, core: 2. Of those that a mesh axis runs over, the one named last changes fastest.
Arguments:
- images: bfloat16 [8, 1024, 1024], P('dp', 'tensor'), may hold values from -6 to 6
- out_grad: bfloat16 [8, 1024, 1024], P('dp', 'tensor'), may hold values from -6 to 6
- live_images: int32 [8], replicated, may hold values from 0 to 1, as said below
- attn_in: bfloat16 [2, 1024, 3, 1024], P('section', None, None, 'tensor'), may hold values from -0.1875 to 0.1875
- qv_bias: float32 [2, 2, 1024], P('section', None, 'tensor'), may hold values from -1.5 to 1.5
- attn_out: bfloat16 [2, 1024, 1024], P('section', 'tensor'), may hold values from -0.75 to 0.75
- mlp_in: bfloat16 [2, 1024, 4096], P('section', None, 'tensor'), may hold values from -0.1875 to 0.1875
- mlp_bias: float32 [2, 4096], P('section', 'tensor'), may hold values from -2.5 to 2.5
- mlp_out: bfloat16 [2, 4096, 1024], P('section', 'tensor'), may hold values from -0.125 to 0.125
- vectors: float32 [2, 8, 1024], P('section'), may hold values from -1.2 to 2
Outputs:
- section_out: bfloat16 [2, 8, 1024, 1024], P('section', 'dp', 'tensor')
- section_in_grad: bfloat16 [2, 8, 1024, 1024], P('section', 'dp', 'tensor')
- attn_in_grad: float32 [2, 1024, 3, 1024], P('section', None, None, 'tensor')
- qv_bias_grad: float32 [2, 2, 1024], P('section', None, 'tensor')
- attn_out_grad: float32 [2, 1024, 1024], P('section', 'tensor')
- mlp_in_grad: float32 [2, 1024, 4096], P('section', None, 'tensor')
- mlp_bias_grad: float32 [2, 4096], P('section', 'tensor')
- mlp_out_grad: float32 [2, 4096, 1024], P('section', 'tensor')
- vectors_grad: float32 [2, 8, 1024], P('section')
Inputs may be any that keep to these rules, and one draw needn't show every extreme that they name: `live_images`: the images of a data group in a micro-batch occupy that micro-batch's first slots of the group; in every micro-batch one data group holds 1 image and another none.
All inputs are finite; a program needn't handle non-finite values.
Results may differ from a plain program's by a relative error of at most 0.018.
Values may be sent and summed in bfloat16 or wider, within the bound.
A program may use at most 128 MiB of HBM per device.

v0:
```python
import jax
import jax.numpy as jnp
from jax import lax
from jax.sharding import PartitionSpec as P

HD = 64
MICRO = 2


EPSILON = 1e-06


def passed_along(value, axis, steps):
    count = lax.axis_size(axis)
    initial, last = (max(0, -steps), min(count, count - steps))
    return lax.ppermute(value, axis, [(source, source + steps) for source in range(initial, last)])


def as_sent(value):
    return jax.tree.map(lambda a: a.astype(jnp.bfloat16) if a.dtype == jnp.float32 else a, value)


def normalize(tokens, gain_vec, offset):
    center = tokens - jnp.mean(tokens, axis=-1, keepdims=True)
    inv_scale = lax.rsqrt(jnp.mean(center * center, axis=-1, keepdims=True) + EPSILON)
    unit_rows = center * inv_scale
    return (unit_rows * gain_vec + offset, unit_rows, inv_scale)


def normalize_back(grad_rows, unit_rows, inv_scale, gain_vec):
    scaled = grad_rows * gain_vec
    return inv_scale * (
        scaled
        - jnp.mean(scaled, axis=-1, keepdims=True)
        - unit_rows * jnp.mean(scaled * unit_rows, axis=-1, keepdims=True)
    )


def exact_gelu(values):
    return jax.nn.gelu(values, approximate=False)


def split_blocks(values, block_rows):
    count, length = (values.shape[0], values.shape[1])
    return values.reshape((count, length // block_rows, block_rows) + values.shape[2:]).swapaxes(
        0, 1
    )


def join_blocks(values):
    merged = values.swapaxes(0, 1)
    return merged.reshape((merged.shape[0], merged.shape[1] * merged.shape[2]) + merged.shape[3:])


def attend(queries, keys_in, values):
    block_rows = min(512, queries.shape[1])
    factor = queries.shape[-1] ** (-0.5)

    def score_block(q_block):
        scores = (
            jnp.einsum("pqhe,pkhe->phqk", q_block, keys_in, preferred_element_type=jnp.float32)
            * factor
        )
        row_max = jnp.max(scores, axis=-1, keepdims=True)
        exponent = jnp.exp(scores - row_max)
        row_total = jnp.sum(exponent, axis=-1, keepdims=True)
        shares = (exponent / row_total).astype(jnp.bfloat16)
        block_out = jnp.einsum(
            "phqk,pkhe->pqhe", shares, values, preferred_element_type=jnp.float32
        )
        return (block_out.astype(jnp.bfloat16), (row_max + jnp.log(row_total))[..., 0])

    block_out, log_sums = lax.map(score_block, split_blocks(queries, block_rows))
    return (join_blocks(block_out), log_sums)


def attend_back(queries, keys_in, values, log_sums, d_out):
    block_rows = min(512, queries.shape[1])
    factor = queries.shape[-1] ** (-0.5)

    def grad_block(carry, pieces):
        d_keys, d_values = carry
        q_block, d_block, log_block = pieces
        scores = (
            jnp.einsum("pqhe,pkhe->phqk", q_block, keys_in, preferred_element_type=jnp.float32)
            * factor
        )
        shares = jnp.exp(scores - log_block[..., None])
        d_shares = jnp.einsum(
            "pqhe,pkhe->phqk", d_block, values, preferred_element_type=jnp.float32
        )
        d_scores = (
            shares * (d_shares - jnp.sum(shares * d_shares, axis=-1, keepdims=True))
        ).astype(jnp.bfloat16)
        d_query = (
            jnp.einsum("phqk,pkhe->pqhe", d_scores, keys_in, preferred_element_type=jnp.float32)
            * factor
        )
        d_keys = (
            d_keys
            + jnp.einsum("phqk,pqhe->pkhe", d_scores, q_block, preferred_element_type=jnp.float32)
            * factor
        )
        d_values = d_values + jnp.einsum(
            "phqk,pqhe->pkhe",
            shares.astype(jnp.bfloat16),
            d_block,
            preferred_element_type=jnp.float32,
        )
        return ((d_keys, d_values), d_query)

    zero_keys = jnp.zeros(keys_in.shape, jnp.float32)
    (d_keys, d_values), d_queries = lax.scan(
        grad_block,
        (zero_keys, zero_keys),
        (split_blocks(queries, block_rows), split_blocks(d_out, block_rows), log_sums),
    )
    return (join_blocks(d_queries), d_keys, d_values)


def spread_rows(normed):
    return lax.all_gather(normed, "tensor", axis=1, tiled=True)


def sum_branch(left, weight, form):
    partial_value = jnp.einsum(form, left, weight, preferred_element_type=jnp.float32)
    return lax.psum_scatter(
        partial_value.astype(jnp.bfloat16), "tensor", scatter_dimension=1, tiled=True
    ).astype(jnp.float32)


def spread_grads(grad_rows):
    return lax.all_gather(grad_rows, "tensor", axis=1, tiled=True)


def sum_norm_grads(left, weight, form):
    partial_value = jnp.einsum(form, left, weight, preferred_element_type=jnp.float32)
    return lax.psum_scatter(
        partial_value.astype(jnp.bfloat16), "tensor", scatter_dimension=1, tiled=True
    ).astype(jnp.float32)


def forward_layer(layer_in, weights):
    w_in, qv_bias, w_out, w_up, b_up, w_down, vectors = weights
    residual = layer_in.astype(jnp.float32)
    normed_one, unit_one, scale_one = normalize(residual, vectors[0], vectors[1])
    normed_one = normed_one.astype(jnp.bfloat16)
    whole_one = spread_rows(normed_one)
    mixture = jnp.einsum("pld,dcf->plcf", whole_one, w_in, preferred_element_type=jnp.float32)
    queries = (mixture[:, :, 0] + qv_bias[0]).astype(jnp.bfloat16)
    keys_in = mixture[:, :, 1].astype(jnp.bfloat16)
    values = (mixture[:, :, 2] + qv_bias[1]).astype(jnp.bfloat16)
    head_shape = queries.shape[:2] + (queries.shape[2] // HD, HD)
    attended, log_sums = attend(
        queries.reshape(head_shape), keys_in.reshape(head_shape), values.reshape(head_shape)
    )
    attended = attended.reshape(queries.shape)
    branch = sum_branch(attended, w_out, "plf,fd->pld") + vectors[2]
    hidden = residual + vectors[3] * branch
    normed_two, unit_two, scale_two = normalize(hidden, vectors[4], vectors[5])
    normed_two = normed_two.astype(jnp.bfloat16)
    whole_two = spread_rows(normed_two)
    pre_act = jnp.einsum("pld,df->plf", whole_two, w_up, preferred_element_type=jnp.float32) + b_up
    activated = exact_gelu(pre_act).astype(jnp.bfloat16)
    branch_two = sum_branch(activated, w_down, "plf,fd->pld") + vectors[6]
    result = hidden + vectors[7] * branch_two
    rows_one, rows_two = (whole_one, whole_two)
    kept = (
        unit_one,
        scale_one,
        rows_one,
        queries,
        keys_in,
        values,
        attended,
        log_sums,
        branch,
        unit_two,
        scale_two,
        rows_two,
        pre_act,
        branch_two,
    )
    return (result, kept)


def backward_layer(kept, cotangent, weights):
    w_in, qv_bias, w_out, w_up, b_up, w_down, vectors = weights
    (
        unit_one,
        scale_one,
        rows_one,
        queries,
        keys_in,
        values,
        attended,
        log_sums,
        branch,
        unit_two,
        scale_two,
        rows_two,
        pre_act,
        branch_two,
    ) = kept
    whole_one, whole_two = (rows_one, rows_two)
    token_axes = (0, 1)
    d_branch_two = (cotangent * vectors[7]).astype(jnp.bfloat16)
    g_scale_two = jnp.sum(cotangent * branch_two, axis=token_axes)
    g_bias_down = jnp.sum(d_branch_two.astype(jnp.float32), axis=token_axes)
    d_full_two = spread_grads(d_branch_two)
    activated, gelu_pull = jax.vjp(exact_gelu, pre_act)
    activated = activated.astype(jnp.bfloat16)
    g_down = jnp.einsum("plf,pld->fd", activated, d_full_two, preferred_element_type=jnp.float32)
    d_activated = jnp.einsum("pld,fd->plf", d_full_two, w_down, preferred_element_type=jnp.float32)
    d_pre = gelu_pull(d_activated)[0].astype(jnp.bfloat16)
    g_bias_up = jnp.sum(d_pre.astype(jnp.float32), axis=token_axes)
    g_up = jnp.einsum("pld,plf->df", whole_two, d_pre, preferred_element_type=jnp.float32)
    d_normed_two = sum_norm_grads(d_pre, w_up, "plf,df->pld")
    g_gain_two = jnp.sum(d_normed_two * unit_two, axis=token_axes)
    g_shift_two = jnp.sum(d_normed_two, axis=token_axes)
    d_hidden = cotangent + normalize_back(d_normed_two, unit_two, scale_two, vectors[4])
    d_branch = (d_hidden * vectors[3]).astype(jnp.bfloat16)
    g_scale_one = jnp.sum(d_hidden * branch, axis=token_axes)
    g_bias_out = jnp.sum(d_branch.astype(jnp.float32), axis=token_axes)
    d_full_one = spread_grads(d_branch)
    g_out = jnp.einsum("plf,pld->fd", attended, d_full_one, preferred_element_type=jnp.float32)
    d_attended = jnp.einsum(
        "pld,fd->plf", d_full_one, w_out, preferred_element_type=jnp.float32
    ).astype(jnp.bfloat16)
    head_shape = queries.shape[:2] + (queries.shape[2] // HD, HD)
    d_query, d_keys, d_values = attend_back(
        queries.reshape(head_shape),
        keys_in.reshape(head_shape),
        values.reshape(head_shape),
        log_sums,
        d_attended.reshape(head_shape),
    )
    d_mixture = jnp.stack([d_query, d_keys, d_values], axis=2)
    d_mixture = d_mixture.reshape(queries.shape[:2] + (3, queries.shape[2])).astype(jnp.bfloat16)
    g_qv = jnp.stack(
        [
            jnp.sum(d_mixture[:, :, 0].astype(jnp.float32), axis=token_axes),
            jnp.sum(d_mixture[:, :, 2].astype(jnp.float32), axis=token_axes),
        ]
    )
    g_in = jnp.einsum("pld,plcf->dcf", whole_one, d_mixture, preferred_element_type=jnp.float32)
    d_normed_one = sum_norm_grads(d_mixture, w_in, "plcf,dcf->pld")
    g_gain_one = jnp.sum(d_normed_one * unit_one, axis=token_axes)
    g_shift_one = jnp.sum(d_normed_one, axis=token_axes)
    d_tokens = d_hidden + normalize_back(d_normed_one, unit_one, scale_one, vectors[0])
    g_vectors = jnp.stack(
        [
            g_gain_one,
            g_shift_one,
            g_bias_out,
            g_scale_one,
            g_gain_two,
            g_shift_two,
            g_bias_down,
            g_scale_two,
        ]
    )
    return (d_tokens, (g_in, g_qv, g_out, g_up, g_bias_up, g_down), g_vectors)


def body(
    images, out_grad, live_images, attn_in, qv_bias, attn_out, mlp_in, mlp_bias, mlp_out, vectors
):
    weights = (attn_in[0], qv_bias[0], attn_out[0], mlp_in[0], mlp_bias[0], mlp_out[0], vectors[0])
    on_first = lax.axis_index("section") == 0
    per_batch = images.shape[0] // MICRO
    counts = live_images.reshape(-1, MICRO)
    totals = jnp.sum(counts, axis=0).astype(jnp.float32)
    own_counts = lax.dynamic_index_in_dim(counts, lax.axis_index("dp"), 0, keepdims=False)
    within = jnp.arange(per_batch, dtype=jnp.int32)
    slot_weight = jnp.where(
        within[None, :] < own_counts[:, None], 1.0 / totals[:, None], jnp.float32(0.0)
    )
    batch_shape = (per_batch,) + images.shape[1:]
    incoming = jnp.zeros(batch_shape, jnp.bfloat16)
    outputs, saved = ([], [])
    for timestep in range(MICRO + 1):
        batch_idx = min(timestep, MICRO - 1)
        own_rows = images[batch_idx * per_batch : (batch_idx + 1) * per_batch]
        layer_in = jnp.where(on_first, own_rows, incoming)
        result, kept = forward_layer(layer_in, weights)
        result = result.astype(jnp.bfloat16)
        outputs.append(result)
        saved.append(kept)
        if timestep < MICRO:
            incoming = passed_along(result, "section", 1)
    returned = jnp.zeros(batch_shape, jnp.bfloat16)
    input_grads = []
    grad_totals = None
    vector_total = None
    for timestep in range(MICRO + 1):
        late_idx = MICRO - 1 - timestep
        if late_idx >= 0:
            own_grad = (
                out_grad[late_idx * per_batch : (late_idx + 1) * per_batch].astype(jnp.float32)
                * slot_weight[late_idx][:, None, None]
            )
        else:
            own_grad = jnp.zeros(batch_shape, jnp.float32)
        cotangent = jnp.where(on_first, returned.astype(jnp.float32), own_grad)
        grad_rows, tick_grads, tick_vectors = backward_layer(
            saved[MICRO - timestep], cotangent, weights
        )
        grad_rows = grad_rows.astype(jnp.bfloat16)
        input_grads.append(grad_rows)
        if timestep < MICRO:
            returned = passed_along(grad_rows, "section", -1)
        if grad_totals is None:
            grad_totals, vector_total = (tick_grads, tick_vectors)
        else:
            grad_totals = tuple(
                (total + extra_grad for total, extra_grad in zip(grad_totals, tick_grads))
            )
            vector_total = vector_total + tick_vectors
    grad_totals = jax.tree.map(
        lambda part: part.astype(jnp.float32), lax.psum(as_sent(grad_totals), "dp")
    )
    vector_total = lax.psum(vector_total, ("tensor", "dp"))
    section_rows = [
        jnp.where(on_first, outputs[batch], outputs[batch + 1]) for batch in range(MICRO)
    ]
    grad_parts = [
        jnp.where(on_first, input_grads[MICRO - batch], input_grads[MICRO - 1 - batch])
        for batch in range(MICRO)
    ]
    section_out = jnp.concatenate(section_rows, axis=0)[None]
    section_in_grad = jnp.concatenate(grad_parts, axis=0)[None]
    g_in, g_qv, g_out, g_up, g_bias_up, g_down = grad_totals
    return (
        section_out,
        section_in_grad,
        g_in[None],
        g_qv[None],
        g_out[None],
        g_up[None],
        g_bias_up[None],
        g_down[None],
        vector_total[None],
    )


def solution(mesh):
    placed = (
        P("dp", "tensor", None),
        P("dp", "tensor", None),
        P(),
        P("section", None, None, "tensor"),
        P("section", None, "tensor"),
        P("section", "tensor", None),
        P("section", None, "tensor"),
        P("section", "tensor"),
        P("section", "tensor", None),
        P("section", None, None),
    )
    return jax.shard_map(
        body,
        mesh=mesh,
        in_specs=placed,
        out_specs=(
            P("section", "dp", "tensor", None),
            P("section", "dp", "tensor", None),
            P("section", None, None, "tensor"),
            P("section", None, "tensor"),
            P("section", "tensor", None),
            P("section", None, "tensor"),
            P("section", "tensor"),
            P("section", "tensor", None),
            P("section", None, None),
        ),
        check_vma=False,
    )
```

profile of v0, /device:TPU:6, one launch (start us, length us, event | category | flops | bytes accessed | tf_op | source)
XLA Modules:
  0.0 1997.1 jit_solution(7118268918604742211)
XLA Ops:
  13.1 47.7 %all-gather.13.cloned.1.call-done = bf16[1,1024,1024]{2,1,0:T(8,128)(2,1)} async-done(((bf16[1,64,1024]{2,1,0:T(8,128)(2,1)}), bf16[1,1024,1024]{2,1,0:T(8,128)(2,1)}) %all-gather.13.cloned.1.call-update) | async-done | bytes 2097168 | tf_op jit(solution)/shard_map/all_gather | solution.py:122
  70.0 70.7 %reduce-scatter.13.cloned.1.call-done = bf16[1,64,1024]{2,1,0:T(8,128)(2,1)} async-done(((bf16[1,1024,1024]{2,1,0:T(8,128)(2,1)}), bf16[1,64,1024]{2,1,0:T(8,128)(2,1)}) %reduce-scatter.13.cloned.1.call-update) | async-done | bytes 131088 | tf_op jit(solution)/shard_map/reduce_scatter | solution.py:127
  144.7 45.8 %all-gather.15.cloned.1.call-done = bf16[1,1024,1024]{2,1,0:T(8,128)(2,1)} async-done(((bf16[1,64,1024]{2,1,0:T(8,128)(2,1)}), bf16[1,1024,1024]{2,1,0:T(8,128)(2,1)}) %all-gather.15.cloned.1.call-update) | async-done | bytes 2097168 | tf_op jit(solution)/shard_map/all_gather | solution.py:122
  200.3 70.0 %reduce-scatter.15.cloned.1.call-done = bf16[1,64,1024]{2,1,0:T(8,128)(2,1)} async-done(((bf16[1,1024,1024]{2,1,0:T(8,128)(2,1)}), bf16[1,64,1024]{2,1,0:T(8,128)(2,1)}) %reduce-scatter.15.cloned.1.call-update) | async-done | bytes 131088 | tf_op jit(solution)/shard_map/reduce_scatter | solution.py:127
  281.3 45.6 %all-gather.17.cloned.1.call-done = bf16[1,1024,1024]{2,1,0:T(8,128)(2,1)} async-done(((bf16[1,64,1024]{2,1,0:T(8,128)(2,1)}), bf16[1,1024,1024]{2,1,0:T(8,128)(2,1)}) %all-gather.17.cloned.1.call-update) | async-done | bytes 2097168 | tf_op jit(solution)/shard_map/all_gather | solution.py:122
  335.6 70.8 %reduce-scatter.17.cloned.1.call-done = bf16[1,64,1024]{2,1,0:T(8,128)(2,1)} async-done(((bf16[1,1024,1024]{2,1,0:T(8,128)(2,1)}), bf16[1,64,1024]{2,1,0:T(8,128)(2,1)}) %reduce-scatter.17.cloned.1.call-update) | async-done | bytes 131088 | tf_op jit(solution)/shard_map/reduce_scatter | solution.py:127
  410.5 45.6 %all-gather.19.cloned.1.call-done = bf16[1,1024,1024]{2,1,0:T(8,128)(2,1)} async-done(((bf16[1,64,1024]{2,1,0:T(8,128)(2,1)}), bf16[1,1024,1024]{2,1,0:T(8,128)(2,1)}) %all-gather.19.cloned.1.call-update) | async-done | bytes 2097168 | tf_op jit(solution)/shard_map/all_gather | solution.py:122
  465.0 70.8 %reduce-scatter.19.cloned.1.call-done = bf16[1,64,1024]{2,1,0:T(8,128)(2,1)} async-done(((bf16[1,1024,1024]{2,1,0:T(8,128)(2,1)}), bf16[1,64,1024]{2,1,0:T(8,128)(2,1)}) %reduce-scatter.19.cloned.1.call-update) | async-done | bytes 131088 | tf_op jit(solution)/shard_map/reduce_scatter | solution.py:127
  545.6 45.5 %all-gather.21.cloned.1.call-done = bf16[1,1024,1024]{2,1,0:T(8,128)(2,1)} async-done(((bf16[1,64,1024]{2,1,0:T(8,128)(2,1)}), bf16[1,1024,1024]{2,1,0:T(8,128)(2,1)}) %all-gather.21.cloned.1.call-update) | async-done | bytes 2097168 | tf_op jit(solution)/shard_map/all_gather | solution.py:122
  600.4 70.8 %reduce-scatter.21.cloned.1.call-done = bf16[1,64,1024]{2,1,0:T(8,128)(2,1)} async-done(((bf16[1,1024,1024]{2,1,0:T(8,128)(2,1)}), bf16[1,64,1024]{2,1,0:T(8,128)(2,1)}) %reduce-scatter.21.cloned.1.call-update) | async-done | bytes 131088 | tf_op jit(solution)/shard_map/reduce_scatter | solution.py:127
  675.7 45.3 %all-gather.23.cloned.1.call-done = bf16[1,1024,1024]{2,1,0:T(8,128)(2,1)} async-done(((bf16[1,64,1024]{2,1,0:T(8,128)(2,1)}), bf16[1,1024,1024]{2,1,0:T(8,128)(2,1)}) %all-gather.23.cloned.1.call-update) | async-done | bytes 2097168 | tf_op jit(solution)/shard_map/all_gather | solution.py:122
  727.0 43.6 %all-gather.25.cloned.1.call-done = bf16[1,1024,1024]{2,1,0:T(8,128)(2,1)} async-done(((bf16[1,64,1024]{2,1,0:T(8,128)(2,1)}), bf16[1,1024,1024]{2,1,0:T(8,128)(2,1)}) %all-gather.25.cloned.1.call-update) | async-done | bytes 2097168 | tf_op jit(solution)/shard_map/all_gather | solution.py:133
  777.3 70.8 %reduce-scatter.25.cloned.1.call-done = bf16[1,64,1024]{2,1,0:T(8,128)(2,1)} async-done(((bf16[1,1024,1024]{2,1,0:T(8,128)(2,1)}), bf16[1,64,1024]{2,1,0:T(8,128)(2,1)}) %reduce-scatter.25.cloned.1.call-update) | async-done | bytes 131088 | tf_op jit(solution)/shard_map/reduce_scatter | solution.py:138
  853.3 45.4 %all-gather.27.cloned.1.call-done = bf16[1,1024,1024]{2,1,0:T(8,128)(2,1)} async-done(((bf16[1,64,1024]{2,1,0:T(8,128)(2,1)}), bf16[1,1024,1024]{2,1,0:T(8,128)(2,1)}) %all-gather.27.cloned.1.call-update) | async-done | bytes 2097168 | tf_op jit(solution)/shard_map/all_gather | solution.py:133
  918.1 70.8 %reduce-scatter.27.cloned.1.call-done = bf16[1,64,1024]{2,1,0:T(8,128)(2,1)} async-done(((bf16[1,1024,1024]{2,1,0:T(8,128)(2,1)}), bf16[1,64,1024]{2,1,0:T(8,128)(2,1)}) %reduce-scatter.27.cloned.1.call-update) | async-done | bytes 131088 | tf_op jit(solution)/shard_map/reduce_scatter | solution.py:138
  999.0 47.3 %all-gather.29.cloned.1.call-done = bf16[1,1024,1024]{2,1,0:T(8,128)(2,1)} async-done(((bf16[1,64,1024]{2,1,0:T(8,128)(2,1)}), bf16[1,1024,1024]{2,1,0:T(8,128)(2,1)}) %all-gather.29.cloned.1.call-update) | async-done | bytes 2097168 | tf_op jit(solution)/shard_map/all_gather | solution.py:133
  1053.0 70.8 %reduce-scatter.29.cloned.1.call-done = bf16[1,64,1024]{2,1,0:T(8,128)(2,1)} async-done(((bf16[1,1024,1024]{2,1,0:T(8,128)(2,1)}), bf16[1,64,1024]{2,1,0:T(8,128)(2,1)}) %reduce-scatter.29.cloned.1.call-update) | async-done | bytes 131088 | tf_op jit(solution)/shard_map/reduce_scatter | solution.py:138
  1128.7 45.8 %all-gather.31.cloned.1.call-done = bf16[1,1024,1024]{2,1,0:T(8,128)(2,1)} async-done(((bf16[1,64,1024]{2,1,0:T(8,128)(2,1)}), bf16[1,1024,1024]{2,1,0:T(8,128)(2,1)}) %all-gather.31.cloned.1.call-update) | async-done | bytes 2097168 | tf_op jit(solution)/shard_map/all_gather | solution.py:133
  1195.5 68.6 %reduce-scatter.31.cloned.1.call-done = bf16[1,64,1024]{2,1,0:T(8,128)(2,1)} async-done(((bf16[1,1024,1024]{2,1,0:T(8,128)(2,1)}), bf16[1,64,1024]{2,1,0:T(8,128)(2,1)}) %reduce-scatter.31.cloned.1.call-update) | async-done | bytes 131088 | tf_op jit(solution)/shard_map/reduce_scatter | solution.py:138
  1270.3 68.1 %reduce-scatter.23.cloned.1.call-done = bf16[1,64,1024]{2,1,0:T(8,128)(2,1)} async-done(((bf16[1,1024,1024]{2,1,0:T(8,128)(2,1)}), bf16[1,64,1024]{2,1,0:T(8,128)(2,1)}) %reduce-scatter.23.cloned.1.call-update) | async-done | bytes 131088 | tf_op jit(solution)/shard_map/reduce_scatter | solution.py:127
  1342.3 45.7 %all-gather.33.cloned.1.call-done = bf16[1,1024,1024]{2,1,0:T(8,128)(2,1)} async-done(((bf16[1,64,1024]{2,1,0:T(8,128)(2,1)}), bf16[1,1024,1024]{2,1,0:T(8,128)(2,1)}) %all-gather.33.cloned.1.call-update) | async-done | bytes 2097168 | tf_op jit(solution)/shard_map/all_gather | solution.py:133
  1393.9 70.8 %reduce-scatter.33.cloned.1.call-done = bf16[1,64,1024]{2,1,0:T(8,128)(2,1)} async-done(((bf16[1,1024,1024]{2,1,0:T(8,128)(2,1)}), bf16[1,64,1024]{2,1,0:T(8,128)(2,1)}) %reduce-scatter.33.cloned.1.call-update) | async-done | bytes 131088 | tf_op jit(solution)/shard_map/reduce_scatter | solution.py:138
  1593.0 67.8 %reduce-scatter.35.cloned.1.call-done = bf16[1,64,1024]{2,1,0:T(8,128)(2,1)} async-done(((bf16[1,1024,1024]{2,1,0:T(8,128)(2,1)}), bf16[1,64,1024]{2,1,0:T(8,128)(2,1)}) %reduce-scatter.35.cloned.1.call-update) | async-done | bytes 131088 | tf_op jit(solution)/shard_map/reduce_scatter | solution.py:138
  1662.2 326.4 %psum.55 = f32[1,8,1024]{2,1,0:T(8,128)} all-reduce(f32[1,8,1024]{2,1,0:T(8,128)S(1)} %add_bitcast_fusion), channel_id=1, replica_groups=mesh['section'=2,'tensor'=16,'dp'=4] {'tensor','dp'}, use_global_device_ids=true, to_apply=%region_97.98 | all-reduce | flops 8192 | bytes 65536 | tf_op jit(solution)/shard_map/psum | solution.py:323
  (654 shorter events, 343.7 us)
Async XLA Ops:
  12.3 128.5 %reduce-scatter.13.cloned.1.call-start = ((), (), s32[]{:S(2)}) async-start(), calls=%async_computation.13 | async-start | bytes 2228224 | tf_op jit(solution)/shard_map/reduce_scatter | solution.py:127
  70.0 120.6 %all-gather.15.cloned.1.call-start = ((), (), s32[]{:S(2)}) async-start(), calls=%async_computation.14 | async-start | bytes 2228224 | tf_op jit(solution)/shard_map/all_gather | solution.py:122
  144.7 125.6 %reduce-scatter.15.cloned.1.call-start = ((), (), s32[]{:S(2)}) async-start(), calls=%async_computation.15 | async-start | bytes 2228224 | tf_op jit(solution)/shard_map/reduce_scatter | solution.py:127
  199.5 127.4 %all-gather.17.cloned.1.call-start = ((), (), s32[]{:S(2)}) async-start(), calls=%async_computation.16 | async-start | bytes 2228224 | tf_op jit(solution)/shard_map/all_gather | solution.py:122
  281.2 125.1 %reduce-scatter.17.cloned.1.call-start = ((), (), s32[]{:S(2)}) async-start(), calls=%async_computation.17 | async-start | bytes 2228224 | tf_op jit(solution)/shard_map/reduce_scatter | solution.py:127
  335.6 120.6 %all-gather.19.cloned.1.call-start = ((), (), s32[]{:S(2)}) async-start(), calls=%async_computation.18 | async-start | bytes 2228224 | tf_op jit(solution)/shard_map/all_gather | solution.py:122
  410.3 125.5 %reduce-scatter.19.cloned.1.call-start = ((), (), s32[]{:S(2)}) async-start(), calls=%async_computation.19 | async-start | bytes 2228224 | tf_op jit(solution)/shard_map/reduce_scatter | solution.py:127
  465.0 126.2 %all-gather.21.cloned.1.call-start = ((), (), s32[]{:S(2)}) async-start(), calls=%async_computation.20 | async-start | bytes 2228224 | tf_op jit(solution)/shard_map/all_gather | solution.py:122
  545.5 125.7 %reduce-scatter.21.cloned.1.call-start = ((), (), s32[]{:S(2)}) async-start(), calls=%async_computation.21 | async-start | bytes 2228224 | tf_op jit(solution)/shard_map/reduce_scatter | solution.py:127
  600.3 120.6 %all-gather.23.cloned.1.call-start = ((), (), s32[]{:S(2)}) async-start(), calls=%async_computation.22 | async-start | bytes 2228224 | tf_op jit(solution)/shard_map/all_gather | solution.py:122
  675.1 95.5 %all-gather.25.cloned.1.call-start = ((), (), s32[]{:S(2)}) async-start(), calls=%async_computation.24 | async-start | bytes 2228224 | tf_op jit(solution)/shard_map/all_gather | solution.py:133
  675.7 172.4 %reduce-scatter.25.cloned.1.call-start = ((), (), s32[]{:S(2)}) async-start(), calls=%async_computation.25 | async-start | bytes 2228224 | tf_op jit(solution)/shard_map/reduce_scatter | solution.py:138
  777.2 121.5 %all-gather.27.cloned.1.call-start = ((), (), s32[]{:S(2)}) async-start(), calls=%async_computation.26 | async-start | bytes 2228224 | tf_op jit(solution)/shard_map/all_gather | solution.py:133
  852.8 136.1 %reduce-scatter.27.cloned.1.call-start = ((), (), s32[]{:S(2)}) async-start(), calls=%async_computation.27 | async-start | bytes 2228224 | tf_op jit(solution)/shard_map/reduce_scatter | solution.py:138
  918.0 128.3 %all-gather.29.cloned.1.call-start = ((), (), s32[]{:S(2)}) async-start(), calls=%async_computation.28 | async-start | bytes 2228224 | tf_op jit(solution)/shard_map/all_gather | solution.py:133
  998.9 124.9 %reduce-scatter.29.cloned.1.call-start = ((), (), s32[]{:S(2)}) async-start(), calls=%async_computation.29 | async-start | bytes 2228224 | tf_op jit(solution)/shard_map/reduce_scatter | solution.py:138
  1053.0 121.5 %all-gather.31.cloned.1.call-start = ((), (), s32[]{:S(2)}) async-start(), calls=%async_computation.30 | async-start | bytes 2228224 | tf_op jit(solution)/shard_map/all_gather | solution.py:133
  1128.6 135.5 %reduce-scatter.31.cloned.1.call-start = ((), (), s32[]{:S(2)}) async-start(), calls=%async_computation.31 | async-start | bytes 2228224 | tf_op jit(solution)/shard_map/reduce_scatter | solution.py:138
  1193.2 145.1 %reduce-scatter.23.cloned.1.call-start = ((), (), s32[]{:S(2)}) async-start(), calls=%async_computation.23 | async-start | bytes 2228224 | tf_op jit(solution)/shard_map/reduce_scatter | solution.py:127
  1195.5 192.5 %all-gather.33.cloned.1.call-start = ((), (), s32[]{:S(2)}) async-start(), calls=%async_computation.32 | async-start | bytes 2228224 | tf_op jit(solution)/shard_map/all_gather | solution.py:133
  1342.1 122.6 %reduce-scatter.33.cloned.1.call-start = ((), (), s32[]{:S(2)}) async-start(), calls=%async_computation.33 | async-start | bytes 2228224 | tf_op jit(solution)/shard_map/reduce_scatter | solution.py:138
  1393.9 120.9 %all-gather.35.cloned.1.call-start = ((), (), s32[]{:S(2)}) async-start(), calls=%async_computation.34 | async-start | bytes 2228224 | tf_op jit(solution)/shard_map/all_gather | solution.py:133
  1469.0 117.1 %all-reduce.4.cloned.1.call-start = ((), (), s32[]{:S(2)}) async-start(), calls=%async_computation.36 | async-start | bytes 3145728 | tf_op jit(solution)/shard_map/psum | solution.py:321
  1534.7 126.2 %reduce-scatter.35.cloned.1.call-start = ((), (), s32[]{:S(2)}) async-start(), calls=%async_computation.35 | async-start | bytes 2228224 | tf_op jit(solution)/shard_map/reduce_scatter | solution.py:138
  (174 other events, 8106.1 us)
Sparse Core Ops, SparseCore 0:
  12.4 48.3 all-gather.12
  70.1 70.6 reduce-scatter.12
  144.8 45.7 all-gather.14
  199.6 70.6 reduce-scatter.14
  281.4 45.4 all-gather.16
  335.7 70.6 reduce-scatter.16
  410.4 45.7 all-gather.18
  465.1 70.6 reduce-scatter.18
  600.5 70.6 reduce-scatter.20
  675.2 45.7 all-gather.22
  724.2 46.3 all-gather.24
  777.3 70.6 reduce-scatter.24
  852.9 45.7 all-gather.26
  918.1 70.6 reduce-scatter.26
  999.0 47.2 all-gather.28
  1053.1 70.6 reduce-scatter.28
  1128.7 45.7 all-gather.30
  1193.3 70.6 reduce-scatter.30
  1268.3 70.0 reduce-scatter.22
  1342.2 45.7 all-gather.32
  1394.0 70.6 reduce-scatter.32
  1469.1 45.7 all-gather.34
  1534.7 51.3 all-reduce.3
  1590.5 70.3 reduce-scatter.34
  (1 shorter events, 45.4 us)
where the time goes:
time: 2010 us; the launch traced here: 2000 us
  waiting for transfers between devices  1420 us (71%)
  blocking collectives  337 us (17%)
  matrix products  107 us (5%)
  other arithmetic  71.5 us (4%)
  local copies, waits for them, and re-layouts  32 us (2%)
    reduce_scatter x6, waiting for transfers between devices, sum_branch(): lax.psum_scatter(partial_value.astype(jnp.bfloat16), 'tensor', scatter_di...  421 us
    reduce_scatter x6, waiting for transfers between devices, sum_norm_grads(): lax.psum_scatter(partial_value.astype(jnp.bfloat16), 'tensor', scatter_di...  420 us
    psum x1, blocking collectives, body(): vector_total = lax.psum(vector_total, ('tensor', 'dp'))  326 us
    all_gather x6, waiting for transfers between devices, spread_rows(): return lax.all_gather(normed, 'tensor', axis=1, tiled=True)  276 us
    all_gather x6, waiting for transfers between devices, spread_grads(): return lax.all_gather(grad_rows, 'tensor', axis=1, tiled=True)  257 us
  transfers between devices with their start and end apart: 29, of which 28 were waited for; matrix products, arithmetic and copies ran while one was open for 2% of the time, Pallas kernels for 0%

commit v1 on v0

v1 whole, which is shorter than its diff:
```python
import jax
import jax.numpy as jnp
from jax import lax
from jax.experimental import pallas as pl
from jax.experimental.pallas import tpu as pltpu
from jax.sharding import PartitionSpec as P

MESH = pl.DeviceIdType.MESH
F32 = jnp.float32
BF16 = jnp.bfloat16
EPSILON = 1e-06
D = 1024
MICRO = 2
LANE = 8
ROWS = 64
PAIRS = LANE // 2
DP = 4
BIAS_ROW = 8
GATHERS = 4
SMALL, QKV, OUT, UP, DOWN = range(5)


def dot_nn(a, b):
    return lax.dot_general(a, b, (((1,), (0,)), ((), ())), preferred_element_type=F32)


def dot_nt(a, b):
    return lax.dot_general(a, b, (((1,), (1,)), ((), ())), preferred_element_type=F32)


def dot_tn(a, b):
    return lax.dot_general(a, b, (((0,), (0,)), ((), ())), preferred_element_type=F32)


def normalize(rows):
    center = rows - jnp.mean(rows, axis=-1, keepdims=True)
    inv = lax.rsqrt(jnp.mean(center * center, axis=-1, keepdims=True) + EPSILON)
    return center * inv, inv


def normalize_back(grad, unit, inv, gain):
    scaled = grad * gain
    return inv * (
        scaled
        - jnp.mean(scaled, axis=-1, keepdims=True)
        - unit * jnp.mean(scaled * unit, axis=-1, keepdims=True)
    )


def sum_rows(rows):
    return jnp.sum(rows, axis=0, keepdims=True)


def kernel(
    x_in, cot_in, small_in, qkv_in, out_in, up_in, down_in,
    so_ref, ig_ref, gw_ref, sm_ref,
    small_w, qkv_w, out_w, up_w, down_w,
    gathered, parts, landed,
    xs, units, invs, branches, hidden, cot,
    queries, kv, attended, probs, act, slope, d_pre, d_mix, d_kv, d_kv_in, d_att,
    grad_m, grad_a, core_m, core_a, mine_m, mine_a, recv_m, recv_a, full_m, full_a,
    vec, lane_vec, core_vec, group_vec, outs, outs_in,
    w_local, w_send, w_recv, ag_send, ag_recv, rs_send, rs_recv,
    kv_send, kv_recv, core_send, core_recv, pair_send, pair_recv, dp_send, dp_recv,
    out_send, out_recv, lane_send, lane_recv, cv_send, cv_recv, gv_send, gv_recv,
):
    section = lax.axis_index("section")
    group = lax.axis_index("dp")
    tensor = lax.axis_index("tensor")
    core = lax.rem(tensor, 2)
    lane = tensor // 2
    own_pair = lane // 2
    other = 1 - core
    member = section * DP + group

    def chip(index):
        return {"tensor": index * 2 + core}

    to_core = {"tensor": lane * 2 + other}
    to_section = {"section": 1 - section}

    def ahead(step):
        return lax.rem(lane + step, LANE)

    def remote(src, dst, send_sem, recv_sem, device):
        return pltpu.make_async_remote_copy(
            src_ref=src, dst_ref=dst, send_sem=send_sem, recv_sem=recv_sem,
            device_id=device, device_id_type=MESH,
        )

    barrier = pltpu.get_barrier_semaphore()
    for step in range(1, LANE):
        pl.semaphore_signal(barrier, inc=1, device_id=chip(ahead(step)), device_id_type=MESH)
    pl.semaphore_signal(barrier, inc=1, device_id=to_core, device_id_type=MESH)
    for step in range(1, 2 * DP):
        friend = lax.rem(member + step, 2 * DP)
        pl.semaphore_signal(
            barrier, inc=1, device_id={"section": friend // DP, "dp": lax.rem(friend, DP)},
            device_id_type=MESH,
        )
    pl.semaphore_wait(barrier, LANE - 1 + 1 + 2 * DP - 1)

    def piece(kind, layer, whose):
        return (
            small_w.at[layer, whose], qkv_w.at[layer, :, whose], out_w.at[layer, whose],
            up_w.at[layer, whose], down_w.at[layer, whose],
        )[kind]

    sources = (small_in, qkv_in, out_in, up_in, down_in)

    def local_piece(kind):
        return pltpu.make_async_copy(sources[kind], piece(kind, section, core), w_local.at[kind])

    def core_piece(kind):
        return remote(sources[kind], piece(kind, section, core),
                      w_send.at[0, kind], w_recv.at[0, kind], to_core)

    def section_piece(kind):
        return remote(sources[kind], piece(kind, section, core),
                      w_send.at[1, kind], w_recv.at[1, kind], to_section)

    def relay_piece(kind):
        return remote(piece(kind, 1 - section, core), piece(kind, 1 - section, core),
                      w_send.at[2, kind], w_recv.at[2, kind], to_core)

    def arrived_piece(kind, way, layer, whose):
        there = piece(kind, layer, whose)
        return remote(there, there, w_send.at[way, kind], w_recv.at[way, kind], to_core)

    for kind in range(5):
        local_piece(kind).start()
    for kind in range(5):
        section_piece(kind).start()
        core_piece(kind).start()

    def take_pieces(kinds):
        for kind in kinds:
            arrived_piece(kind, 1, 1 - section, core).wait_recv()
            relay_piece(kind).start()
        for kind in kinds:
            local_piece(kind).wait()
            arrived_piece(kind, 0, section, other).wait_recv()
            arrived_piece(kind, 2, 1 - section, other).wait_recv()

    def gather_copy(layer, which, slot, dest):
        block = gathered.at[layer, which, lane]
        return remote(block, block, ag_send.at[slot], ag_recv.at[which, lane], chip(dest))

    def gather_dests():
        found = [own_pair * 2 + 1 - lax.rem(lane, 2)]
        for step in range(1, PAIRS):
            pair = lax.rem(own_pair + PAIRS - step, PAIRS)
            found += [pair * 2, pair * 2 + 1]
        return found

    def gather_start(layer, which, rows):
        gathered[layer, which, lane] = rows
        for slot, dest in enumerate(gather_dests()):
            gather_copy(layer, which, slot, dest).start()

    def gather_finish(layer, which):
        for slot, dest in enumerate(gather_dests()):
            gather_copy(layer, which, slot, dest).wait_send()

    def gather_take(layer, which, pair):
        for side in range(2):
            source = pair * 2 + side

            @pl.when(source != lane)
            def _():
                block = gathered.at[layer, which, source]
                remote(block, block, ag_send.at[0], ag_recv.at[which, source],
                       to_core).wait_recv()

        return gathered[layer, which, pl.ds(pair * 2, 2)].reshape(2 * ROWS, D)

    def whole(layer, which):
        return gathered[layer, which].reshape(LANE * ROWS, D)

    def part_copy(which, dest):
        return remote(parts.at[which % 2, dest], landed.at[which % 2, lane],
                      rs_send.at[dest], rs_recv.at[which, lane], chip(dest))

    def part_start(which, pair, rows):
        parts[which % 2, pl.ds(pair * 2, 2)] = rows.astype(BF16).reshape(2, ROWS, D)
        for side in range(2):
            dest = pair * 2 + side

            @pl.when(dest != lane)
            def _():
                part_copy(which, dest).start()

    def part_sum(which):
        total = parts[which % 2, lane].astype(F32)
        for step in range(1, LANE):
            source = ahead(step)
            block = landed.at[which % 2, source]
            remote(block, block, rs_send.at[source], rs_recv.at[which, source],
                   to_core).wait_recv()
            total = total + landed[which % 2, source].astype(F32)
        for step in range(1, LANE):
            part_copy(which, ahead(step)).wait_send()
        return total

    def each_pair(work, first=0):
        @pl.loop(0, PAIRS)
        def _(step):
            work(lax.rem(own_pair + first + step, PAIRS))

    def pair_rows(pair):
        return pl.ds(pl.multiple_of(pair * 2 * ROWS, 2 * ROWS), 2 * ROWS)

    first_head = lax.broadcasted_iota(jnp.int32, (2 * ROWS, 128), 1) < 64

    def vector(layer, row):
        return small_w[layer, core, row:row + 1]

    def both_biases(layer, first, length):
        row = slice(BIAS_ROW, BIAS_ROW + 1)
        return jnp.concatenate(
            [small_w[layer, 0, row, first:first + length],
             small_w[layer, 1, row, first:first + length]], axis=-1)

    def keep_inv(layer, which, inv):
        invs[layer, which] = jnp.broadcast_to(inv, (ROWS, 128))

    def get_inv(layer, which):
        return invs[layer, which, :, 0:1]

    xs[0] = x_in[...].astype(F32)
    vec[...] = jnp.zeros_like(vec)
    take_pieces((SMALL,))

    @pl.loop(0, 2)
    def _(layer):
        unit, inv = normalize(xs[layer])
        units[layer, 0] = unit
        keep_inv(layer, 0, inv)
        gather_start(layer, 0, (unit * vector(layer, 0) + vector(layer, 1)).astype(BF16))

        @pl.when(layer == 0)
        def _():
            take_pieces((QKV,))

        q_bias = both_biases(layer, 0, 64)
        v_bias = both_biases(layer, 128, 64)

        def project(pair):
            rows = gather_take(layer, 0, pair)
            mixed = dot_nt(rows, qkv_w[layer].reshape(384, D))
            queries[layer, pair_rows(pair)] = (
                (mixed[:, 0:128] + q_bias).astype(BF16).astype(F32) * 0.125).astype(BF16)
            kv[layer, core, pair_rows(pair), 0:128] = mixed[:, 128:256].astype(BF16)
            kv[layer, core, pair_rows(pair), 128:256] = (mixed[:, 256:384] + v_bias).astype(BF16)

        each_pair(project)
        kv_copy = remote(kv.at[layer, core], kv.at[layer, core],
                         kv_send.at[0, layer], kv_recv.at[0, layer], to_core)
        kv_copy.start()

        @pl.when(layer == 0)
        def _():
            take_pieces((OUT,))

        there = kv.at[layer, other]
        remote(there, there, kv_send.at[0, layer], kv_recv.at[0, layer], to_core).wait_recv()

        def attend(pair):
            rows = queries[layer, pair_rows(pair)]
            keys = kv[layer, :, :, 0:128].reshape(2 * LANE * ROWS, 128)
            values = kv[layer, :, :, 128:256].reshape(2 * LANE * ROWS, 128)
            found = []
            for head in range(2):
                mask = first_head if head == 0 else jnp.logical_not(first_head)
                scores = dot_nt(jnp.where(mask, rows, jnp.zeros_like(rows)), keys)
                grown = jnp.exp(scores - jnp.max(scores, axis=-1, keepdims=True))
                share = (grown / jnp.sum(grown, axis=-1, keepdims=True)).astype(BF16)
                probs[layer, head, pair_rows(pair)] = share
                found.append(dot_nn(share, values))
            result = jnp.where(first_head, found[0], found[1]).astype(BF16)
            attended[layer, pair_rows(pair)] = result
            part_start(0, pair, dot_nn(result, out_w[layer].reshape(128, D)))

        each_pair(attend, 1)
        kv_copy.wait_send()
        gather_finish(layer, 0)
        branch = part_sum(0) + vector(layer, 2)
        branches[layer, 0] = branch
        state = xs[layer] + vector(layer, 3) * branch
        hidden[...] = state

        unit, inv = normalize(state)
        units[layer, 1] = unit
        keep_inv(layer, 1, inv)
        gather_start(layer, 1, (unit * vector(layer, 4) + vector(layer, 5)).astype(BF16))

        @pl.when(layer == 0)
        def _():
            take_pieces((UP, DOWN))

        up_bias = both_biases(layer, 256, 256)

        def feed(pair):
            rows = gather_take(layer, 1, pair)
            pre = dot_nt(rows, up_w[layer].reshape(512, D)) + up_bias
            cdf = 0.5 + 0.5 * lax.erf(pre * 0.7071067811865476)
            bell = jnp.exp(-0.5 * pre * pre) * 0.3989422804014327
            value = (pre * cdf).astype(BF16)
            act[layer, pair_rows(pair)] = value
            slope[layer, pair_rows(pair)] = cdf + pre * bell
            part_start(1, pair, dot_nn(value, down_w[layer].reshape(512, D)))

        each_pair(feed)
        gather_finish(layer, 1)
        branch = part_sum(1) + vector(layer, 6)
        branches[layer, 1] = branch
        rounded = (hidden[...] + vector(layer, 7) * branch).astype(BF16)
        outs[0, layer] = rounded

        @pl.when(layer == 0)
        def _():
            xs[1] = rounded.astype(F32)

    def out_copy(which):
        return remote(outs.at[which, 1 - section], outs_in.at[which],
                      out_send.at[which], out_recv.at[which], to_section)

    out_copy(0).start()

    def core_copy(kind, layer):
        source, dest = ((grad_m, core_m), (grad_a, core_a))[kind]
        return remote(source.at[layer, other], dest.at[layer],
                      core_send.at[kind, layer], core_recv.at[kind, layer], to_core)

    def owner_copy(kind, layer, quarter):
        source, dest, length = ((mine_m, recv_m, 128), (mine_a, recv_a, 64))[kind]
        return remote(source.at[layer, pl.ds(quarter * length, length)], dest.at[member],
                      pair_send.at[kind, layer, quarter], pair_recv.at[kind, member],
                      {"section": layer, "dp": quarter})

    def owned(layer, quarter):
        return jnp.logical_and(layer == section, quarter == group)

    def core_sum_and_send(kind, layer):
        there, mine, own = ((core_m, mine_m, grad_m), (core_a, mine_a, grad_a))[kind]
        core_copy(kind, layer).wait_recv()
        mine[layer] = (own[layer, core].astype(F32) + there[layer].astype(F32)).astype(BF16)
        for quarter in range(DP):
            @pl.when(jnp.logical_not(owned(layer, quarter)))
            def _():
                owner_copy(kind, layer, quarter).start()

    cot[...] = cot_in[...]

    @pl.loop(0, 2)
    def _(turn):
        layer = 1 - turn
        above = cot[...]
        d_branch2 = (above * vector(layer, 7)).astype(BF16)
        gather_start(layer, 2, d_branch2)
        vec[layer, 7:8] = sum_rows(above * branches[layer, 1])
        vec[layer, 6:7] = sum_rows(d_branch2.astype(F32))

        def feed_back(pair):
            rows = gather_take(layer, 2, pair)
            d_act = dot_nt(rows, down_w[layer].reshape(512, D))
            back = (d_act * slope[layer, pair_rows(pair)]).astype(BF16)
            d_pre[pair_rows(pair)] = back
            vec[layer, 8:9, 0:512] += sum_rows(back.astype(F32))
            part_start(2, pair, dot_nn(back, up_w[layer].reshape(512, D)))

        each_pair(feed_back)
        gather_finish(layer, 2)
        for whose in range(2):
            units_of = slice(whose * 256, whose * 256 + 256)
            grad_m[layer, whose, 0:256] = dot_tn(d_pre[:, units_of], whole(layer, 1)).astype(BF16)
            grad_m[layer, whose, 256:512] = dot_tn(
                act[layer, :, units_of], whole(layer, 2)).astype(BF16)
        core_copy(0, layer).start()
        d_normed = part_sum(2)
        unit, inv = units[layer, 1], get_inv(layer, 1)
        vec[layer, 4:5] = sum_rows(d_normed * unit)
        vec[layer, 5:6] = sum_rows(d_normed)
        d_hidden = above + normalize_back(d_normed, unit, inv, vector(layer, 4))
        hidden[...] = d_hidden
        d_branch = (d_hidden * vector(layer, 3)).astype(BF16)
        gather_start(layer, 3, d_branch)
        vec[layer, 3:4] = sum_rows(d_hidden * branches[layer, 0])
        vec[layer, 2:3] = sum_rows(d_branch.astype(F32))
        core_sum_and_send(0, layer)
        d_kv[...] = jnp.zeros_like(d_kv)

        def attend_back(pair):
            rows = gather_take(layer, 3, pair)
            d_out = dot_nt(rows, out_w[layer].reshape(128, D)).astype(BF16)
            keys = kv[layer, :, :, 0:128].reshape(2 * LANE * ROWS, 128)
            values = kv[layer, :, :, 128:256].reshape(2 * LANE * ROWS, 128)
            q_rows = queries[layer, pair_rows(pair)]
            found, score_grads, shares, q_heads, d_heads = [], [], [], [], []
            for head in range(2):
                mask = first_head if head == 0 else jnp.logical_not(first_head)
                d_head = jnp.where(mask, d_out, jnp.zeros_like(d_out))
                share = probs[layer, head, pair_rows(pair)]
                d_share = dot_nt(d_head, values)
                wide = share.astype(F32)
                product = wide * d_share
                d_score = (product - wide * jnp.sum(product, axis=-1, keepdims=True)).astype(BF16)
                found.append(dot_nn(d_score, keys))
                score_grads.append(d_score)
                shares.append(share)
                q_heads.append(jnp.where(mask, q_rows, jnp.zeros_like(q_rows)))
                d_heads.append(d_head)
            d_query = (jnp.where(first_head, found[0], found[1]) * 0.125).astype(BF16)
            d_mix[pair_rows(pair), 0:128] = d_query
            vec[layer, 9:10, 0:128] += sum_rows(d_query.astype(F32))
            d_keys = dot_tn(jnp.concatenate(score_grads, 0), jnp.concatenate(q_heads, 0))
            d_values = dot_tn(jnp.concatenate(shares, 0), jnp.concatenate(d_heads, 0))
            d_kv[:, :, 0:128] += d_keys.reshape(2, LANE * ROWS, 128)
            d_kv[:, :, 128:256] += d_values.reshape(2, LANE * ROWS, 128)

        each_pair(attend_back)
        gather_finish(layer, 3)
        kv_back = remote(d_kv.at[other], d_kv_in.at[layer],
                         kv_send.at[1, layer], kv_recv.at[1, layer], to_core)
        kv_back.start()
        grads = dot_tn(attended[layer], whole(layer, 3)).astype(BF16)
        grad_a[layer, 0, 192:256] = grads[0:64]
        grad_a[layer, 1, 192:256] = grads[64:128]
        kv_back.wait_recv()
        totals = (d_kv[core] + d_kv_in[layer]).astype(BF16)
        d_mix[:, 128:384] = totals
        vec[layer, 9:10, 128:256] = sum_rows(totals[:, 128:256].astype(F32))

        def project_back(pair):
            part_start(3, pair, dot_nn(d_mix[pair_rows(pair)], qkv_w[layer].reshape(384, D)))

        each_pair(project_back, 1)
        for third in range(3):
            grads = dot_tn(d_mix[:, third * 128:third * 128 + 128], whole(layer, 0)).astype(BF16)
            grad_a[layer, 0, third * 64:third * 64 + 64] = grads[0:64]
            grad_a[layer, 1, third * 64:third * 64 + 64] = grads[64:128]
        core_copy(1, layer).start()
        kv_back.wait_send()
        d_normed = part_sum(3)
        unit, inv = units[layer, 0], get_inv(layer, 0)
        vec[layer, 0:1] = sum_rows(d_normed * unit)
        vec[layer, 1:2] = sum_rows(d_normed)
        rounded = (hidden[...] + normalize_back(d_normed, unit, inv, vector(layer, 0))).astype(BF16)
        outs[1, layer] = rounded
        cot[...] = rounded.astype(F32)
        core_sum_and_send(1, layer)

    out_copy(1).start()

    def lane_copy(dest):
        return remote(vec.at[:, pl.ds(0, 8)], lane_vec.at[lane],
                      lane_send.at[dest], lane_recv.at[lane], chip(dest))

    for step in range(1, LANE):
        lane_copy(ahead(step)).start()
    for step in range(1, LANE):
        source = ahead(step)
        remote(vec.at[:, pl.ds(0, 8)], lane_vec.at[source],
               lane_send.at[source], lane_recv.at[source], to_core).wait_recv()
    for step in range(1, LANE):
        lane_copy(ahead(step)).wait_send()
    for step in range(1, LANE):
        vec[:, 0:8] += lane_vec[ahead(step)]
    cv_copy = remote(vec, core_vec, cv_send.at[0], cv_recv.at[0], to_core)
    cv_copy.start()
    cv_copy.wait()
    vec[...] += core_vec[...]

    def group_copy(layer, quarter):
        return remote(vec.at[layer], group_vec.at[member], gv_send.at[layer, quarter],
                      gv_recv.at[member], {"section": layer, "dp": quarter})

    for layer in range(2):
        for quarter in range(DP):
            @pl.when(jnp.logical_not(owned(layer, quarter)))
            def _():
                group_copy(layer, quarter).start()

    def full_copy(kind, dest):
        ref = (full_m, full_a)[kind]
        return remote(ref.at[group], ref.at[group], dp_send.at[kind, dest],
                      dp_recv.at[kind, group], {"dp": dest})

    for kind in range(2):
        mine, recv, full, length = ((mine_m, recv_m, full_m, 128),
                                    (mine_a, recv_a, full_a, 64))[kind]
        for step in range(1, 2 * DP):
            source = lax.rem(member + step, 2 * DP)
            block = recv.at[source]
            remote(block, block, dp_send.at[kind, 0], pair_recv.at[kind, source],
                   to_core).wait_recv()
        total = mine[section, pl.ds(pl.multiple_of(group * length, length), length)].astype(F32)
        for step in range(1, 2 * DP):
            total = total + recv[lax.rem(member + step, 2 * DP)].astype(F32)
        full[group] = total.astype(BF16)
        for step in range(1, DP):
            full_copy(kind, lax.rem(group + step, DP)).start()

    for step in range(1, 2 * DP):
        source = lax.rem(member + step, 2 * DP)
        block = group_vec.at[source]
        remote(block, block, gv_send.at[0, 0], gv_recv.at[source], to_core).wait_recv()
    total = vec[section]
    for step in range(1, 2 * DP):
        total = total + group_vec[lax.rem(member + step, 2 * DP)]
    sm_ref[...] = total

    for which, ref in ((0, so_ref), (1, ig_ref)):
        out_copy(which).wait()
        ref[section] = outs[which, section]
        ref[1 - section] = outs_in[which]

    for kind in range(2):
        full, length, base = ((full_m, 128, 0), (full_a, 64, 512))[kind]
        for step in range(1, DP):
            source = lax.rem(group + step, DP)
            block = full.at[source]
            remote(block, block, dp_send.at[kind, source], dp_recv.at[kind, source],
                   to_core).wait_recv()
        gw_ref[base:base + DP * length] = full[...].reshape(DP * length, D).astype(F32)

    for kind in range(5):
        core_piece(kind).wait_send()
        section_piece(kind).wait_send()
        relay_piece(kind).wait_send()
    for kind in range(2):
        for step in range(1, DP):
            full_copy(kind, lax.rem(group + step, DP)).wait_send()
        for layer in range(2):
            core_copy(kind, layer).wait_send()
            for quarter in range(DP):
                @pl.when(jnp.logical_not(owned(layer, quarter)))
                def _():
                    owner_copy(kind, layer, quarter).wait_send()
    for layer in range(2):
        for quarter in range(DP):
            @pl.when(jnp.logical_not(owned(layer, quarter)))
            def _():
                group_copy(layer, quarter).wait_send()


def run_layers(x_rows, cot_rows, small, qkv, out, up, down):
    vmem = pl.BlockSpec(memory_space=pltpu.VMEM)
    anywhere = pl.BlockSpec(memory_space=pl.ANY)
    dma = pltpu.SemaphoreType.DMA
    tokens = LANE * ROWS
    scratch = [
        pltpu.VMEM((2, 2, 16, D), F32),
        pltpu.VMEM((2, 3, 2, 64, D), BF16),
        pltpu.VMEM((2, 2, 64, D), BF16),
        pltpu.VMEM((2, 2, 256, D), BF16),
        pltpu.VMEM((2, 2, 256, D), BF16),
        pltpu.VMEM((2, GATHERS, LANE, ROWS, D), BF16),
        pltpu.VMEM((2, LANE, ROWS, D), BF16),
        pltpu.VMEM((2, LANE, ROWS, D), BF16),
        pltpu.VMEM((2, ROWS, D), F32),
        pltpu.VMEM((2, 2, ROWS, D), F32),
        pltpu.VMEM((2, 2, ROWS, 128), F32),
        pltpu.VMEM((2, 2, ROWS, D), F32),
        pltpu.VMEM((ROWS, D), F32),
        pltpu.VMEM((ROWS, D), F32),
        pltpu.VMEM((2, tokens, 128), BF16),
        pltpu.VMEM((2, 2, tokens, 256), BF16),
        pltpu.VMEM((2, tokens, 128), BF16),
        pltpu.VMEM((2, 2, tokens, 2 * tokens), BF16),
        pltpu.VMEM((2, tokens, 512), BF16),
        pltpu.VMEM((2, tokens, 512), F32),
        pltpu.VMEM((tokens, 512), BF16),
        pltpu.VMEM((tokens, 384), BF16),
        pltpu.VMEM((2, tokens, 256), F32),
        pltpu.VMEM((2, tokens, 256), F32),
        pltpu.VMEM((16, 128), F32),
        pltpu.VMEM((2, 2, 512, D), BF16),
        pltpu.VMEM((2, 2, 256, D), BF16),
        pltpu.VMEM((2, 512, D), BF16),
        pltpu.VMEM((2, 256, D), BF16),
        pltpu.VMEM((2, 512, D), BF16),
        pltpu.VMEM((2, 256, D), BF16),
        pltpu.VMEM((2 * DP, 128, D), BF16),
        pltpu.VMEM((2 * DP, 64, D), BF16),
        pltpu.VMEM((DP, 128, D), BF16),
        pltpu.VMEM((DP, 64, D), BF16),
        pltpu.VMEM((2, 16, D), F32),
        pltpu.VMEM((LANE, 2, 8, D), F32),
        pltpu.VMEM((2, 16, D), F32),
        pltpu.VMEM((2 * DP, 16, D), F32),
        pltpu.VMEM((2, 2, ROWS, D), BF16),
        pltpu.VMEM((2, ROWS, D), BF16),
        dma((5,)), dma((3, 5)), dma((3, 5)),
        dma((LANE,)), dma((GATHERS, LANE)),
        dma((LANE,)), dma((GATHERS, LANE)),
        dma((2, 2)), dma((2, 2)),
        dma((2, 2)), dma((2, 2)),
        dma((2, 2, DP)), dma((2, 2 * DP)),
        dma((2, DP)), dma((2, DP)),
        dma((2,)), dma((2,)),
        dma((LANE,)), dma((LANE,)),
        dma((1,)), dma((1,)),
        dma((2, DP)), dma((2 * DP,)),
    ]
    return pl.pallas_call(
        kernel,
        out_shape=(
            jax.ShapeDtypeStruct((2, ROWS, D), BF16),
            jax.ShapeDtypeStruct((2, ROWS, D), BF16),
            jax.ShapeDtypeStruct((768, D), F32),
            jax.ShapeDtypeStruct((16, D), F32),
        ),
        in_specs=[vmem, vmem] + [anywhere] * 5,
        out_specs=(vmem,) * 4,
        scratch_shapes=scratch,
        name="two_layers",
        compiler_params=pltpu.CompilerParams(
            collective_id=0, has_side_effects=True, vmem_limit_bytes=63 * 2**20
        ),
    )(x_rows, cot_rows, small, qkv, out, up, down)


def body(
    images, out_grad, live_images, attn_in, qv_bias, attn_out, mlp_in, mlp_bias, mlp_out, vectors
):
    section = lax.axis_index("section")
    core = lax.rem(lax.axis_index("tensor"), 2)
    counts = live_images.reshape(-1, MICRO)
    totals = jnp.sum(counts, axis=0).astype(F32)
    own = lax.dynamic_slice(counts, (lax.axis_index("dp"), section), (1, 1))[0, 0]
    weight = jnp.where(own > 0, 1.0 / totals[section], F32(0.0))
    x_rows = lax.dynamic_index_in_dim(images, section, 0, keepdims=False)
    cot_rows = lax.dynamic_index_in_dim(out_grad, section, 0, keepdims=False).astype(F32) * weight
    gap = jnp.zeros((64,), F32)
    biases = jnp.concatenate(
        [qv_bias[0, 0], gap, qv_bias[0, 1], gap, mlp_bias[0], jnp.zeros((512,), F32)])
    small = jnp.concatenate([vectors[0], biases[None], jnp.zeros((7, D), F32)], axis=0)
    qkv = attn_in[0].transpose(1, 2, 0)
    up = mlp_in[0].T
    section_out, section_in_grad, grads, sums = run_layers(
        x_rows, cot_rows, small, qkv, attn_out[0], up, mlp_out[0])
    g_in = grads[512:704].reshape(3, 64, D).transpose(2, 0, 1)
    g_up_bias = lax.dynamic_slice(sums, (8, core * 256), (1, 256))
    g_query = lax.dynamic_slice(sums, (9, core * 64), (1, 64))
    g_value = lax.dynamic_slice(sums, (9, 128 + core * 64), (1, 64))
    return (
        section_out[None],
        section_in_grad[None],
        g_in[None],
        jnp.concatenate([g_query, g_value], axis=0)[None],
        grads[704:768][None],
        grads[0:256].T[None],
        g_up_bias,
        grads[256:512][None],
        sums[0:8][None],
    )


def solution(mesh):
    placed = (
        P("dp", "tensor", None),
        P("dp", "tensor", None),
        P(),
        P("section", None, None, "tensor"),
        P("section", None, "tensor"),
        P("section", "tensor", None),
        P("section", None, "tensor"),
        P("section", "tensor"),
        P("section", "tensor", None),
        P("section", None, None),
    )
    return jax.shard_map(
        body,
        mesh=mesh,
        in_specs=placed,
        out_specs=(
            P("section", "dp", "tensor", None),
            P("section", "dp", "tensor", None),
            P("section", None, None, "tensor"),
            P("section", None, "tensor"),
            P("section", "tensor", None),
            P("section", None, "tensor"),
            P("section", "tensor"),
            P("section", "tensor", None),
            P("section", None, None),
        ),
        check_vma=False,
    )
```

time: 2010 us -> 409 us (0.20)
  waiting for transfers between devices: 1420 us -> 0 us
  Pallas kernels: 0 us -> 381 us
  blocking collectives: 337 us -> 0 us
  matrix products: 107 us -> 0 us
  other arithmetic: 71.5 us -> 3.68 us
    reduce_scatter x12 -> x0, waiting for transfers between devices: 841 us -> none  [the longest x6 421 us: sum_branch(): lax.psum_scatter(partial_value.astype(jnp.bfloat16), 'tensor', scatter_di...]
    all_gather x12 -> x0, waiting for transfers between devices: 533 us -> none  [the longest x6 276 us: spread_rows(): return lax.all_gather(normed, 'tensor', axis=1, tiled=True)]
    pallas_call x0 -> x1, Pallas kernels: none -> 381 us  [run_layers(): pl.pallas_call(kernel, out_shape=(jax.ShapeDtypeStruct((2, ROWS, D), BF16...]
    psum x2 -> x0, blocking collectives: 337 us -> none  [the longest x1 326 us: body(): vector_total = lax.psum(vector_total, ('tensor', 'dp'))]
    dot_general x72 -> x0, matrix products: 96.1 us -> none  [the longest x3 17.8 us: forward_layer(): jnp.einsum('pld,df->plf', whole_two, w_up, preferred_element_type=jnp.flo...]
    reduce_sum x35 -> x1, other arithmetic: 39.5 us -> 0.02 us  [body(): totals = jnp.sum(counts, axis=0).astype(F32)]
    psum x1 -> x0, waiting for transfers between devices: 34.5 us -> none  [body(): lax.psum(as_sent(grad_totals), 'dp')]
  transfers between devices with their start and end apart: 29 -> 0, of which waited for: 28 -> 0; matrix products, arithmetic and copies ran while one was open for 2% -> 0% of each run, Pallas kernels for 0% -> 0%
where the time goes in v1:
time: 409 us; the launch traced here: 405 us
  Pallas kernels  381 us (93%)
  local copies, waits for them, and re-layouts  18.9 us (5%)
    pallas_call x1, Pallas kernels, run_layers(): pl.pallas_call(kernel, out_shape=(jax.ShapeDtypeStruct((2, ROWS, D), BF16...  381 us

profile of v1, /device:TPU:6, one launch (start us, length us, event | category | flops | bytes accessed | tf_op | source)
XLA Modules:
  0.0 405.1 jit_solution(68951416354331791)
XLA Ops:
  0.6 0.0 copy-start
  0.7 0.1 pad.4.clone
  0.8 0.8 slice_bitcast_fusion.4
  1.5 0.7 reshape.31
  2.3 0.6 dynamic_slice.24
  3.5 0.6 dynamic_slice.25
  4.8 0.8 concatenate.9
  5.6 1.5 maximum_maximum_fusion.small_in
  7.0 0.0 copy-done
  7.1 0.7 dynamic-slice_bitcast_fusion.x_in
  7.7 1.6 multiply_bitcast_fusion.cot_in
  9.3 2.0 copy.21
  11.4 380.5 %two_layers.1 = (bf16[2,64,1024]{2,1,0:T(8,128)(2,1)}, bf16[2,64,1024]{2,1,0:T(8,128)(2,1)}, f32[768,1024]{1,0:T(8,128)}, f32[16,1024]{1,0:T(8,128)}) custom-call(bf16[64,1024]{1,0:T(8,128)(2,1)} %dynamic-slice_bitcast_fusion.x_in, f32[64,1024]{1,0:T(8,128)} %multiply_bitcast_fusion.cot_in, f32[16,1024]{1,0:T(8,128)} %maximum_maximum_fusion.small_in, ...), custom_call_target="tpu_custom_call" | custom-call | tf_op jit(solution)/shard_map/two_layers/pallas_call | solution.py:606
  391.9 0.8 constant_dynamic-slice_fusion.1
  392.7 0.6 maximum_bitcast_fusion
  393.3 1.3 constant_dynamic-slice_fusion.2
  394.5 1.4 slice_bitcast_fusion.3
  395.9 1.7 slice_bitcast_fusion.2
  397.6 2.1 slice.23
  399.7 2.8 slice_bitcast_fusion
  402.4 1.3 copy.22
  403.7 0.0 copy-done.2
  403.7 0.7 copy.25
  404.4 0.7 copy.26
  (8 shorter events, 0.0 us)
Async XLA Ops:
  0.6 6.4 %copy-start = (bf16[2,64,1024]{2,1,0:T(8,128)(2,1)S(1)}, bf16[2,64,1024]{2,1,0:T(8,128)(2,1)}, u32[]{:S(2)}) copy-start(bf16[2,64,1024]{2,1,0:T(8,128)(2,1)} %param.10) | copy-start | bytes 786436
  399.7 4.1 %copy-start.2 = (bf16[2,64,1024]{2,1,0:T(8,128)(2,1)S(1)}, bf16[2,64,1024]{2,1,0:T(8,128)(2,1)}, u32[]{:S(2)}) copy-start(bf16[2,64,1024]{2,1,0:T(8,128)(2,1)} %get-tuple-element.13) | copy-start | bytes 786436
  399.7 4.8 %copy-start.1 = (bf16[2,64,1024]{2,1,0:T(8,128)(2,1)S(1)}, bf16[2,64,1024]{2,1,0:T(8,128)(2,1)}, u32[]{:S(2)}) copy-start(bf16[2,64,1024]{2,1,0:T(8,128)(2,1)} %get-tuple-element.14) | copy-start | bytes 786436

commit v2 on v1

v2 whole, which is shorter than its diff:
```python
import jax
import jax.numpy as jnp
from jax import lax
from jax.experimental import pallas as pl
from jax.experimental.pallas import tpu as pltpu
from jax.sharding import PartitionSpec as P

MESH = pl.DeviceIdType.MESH
F32 = jnp.float32
BF16 = jnp.bfloat16
EPSILON = 1e-06
D = 1024
MICRO = 2
LANE = 4
QUAD = 4
ROWS = 64
PAIRS = LANE // 2
TOKENS = LANE * ROWS
DP = 4
BIAS_ROW = 8
GATHERS = 4
SMALL, ATTN, MLP = range(3)


def dot_nn(a, b):
    return lax.dot_general(a, b, (((1,), (0,)), ((), ())), preferred_element_type=F32)


def dot_nt(a, b):
    return lax.dot_general(a, b, (((1,), (1,)), ((), ())), preferred_element_type=F32)


def dot_tn(a, b):
    return lax.dot_general(a, b, (((0,), (0,)), ((), ())), preferred_element_type=F32)


def normalize(rows):
    center = rows - jnp.mean(rows, axis=-1, keepdims=True)
    inv = lax.rsqrt(jnp.mean(center * center, axis=-1, keepdims=True) + EPSILON)
    return center * inv, inv


def normalize_back(grad, unit, inv, gain):
    scaled = grad * gain
    return inv * (
        scaled
        - jnp.mean(scaled, axis=-1, keepdims=True)
        - unit * jnp.mean(scaled * unit, axis=-1, keepdims=True)
    )


def sum_rows(rows):
    return jnp.sum(rows, axis=0, keepdims=True)


def kernel(
    x_in, cot_in, small_in, attn_in, mlp_in,
    so_ref, ig_ref, gm_ref, ga_ref, sm_ref,
    small_w, attn_w, mlp_w,
    gathered, parts, landed,
    xs, units, invs, branches, hidden, cot,
    qkv_out, qkv_got, queries, keys, values, att_out, att_got, attended, probs,
    act, slope, d_pre, d_att_got, d_keys, d_values,
    grad_m, grad_a, core_m, core_a, dp_m, dp_a, part_m, part_a, recv_m, recv_a, full_m, full_a,
    vec, lane_vec, core_vec, x_vec, dp_vec, outs, outs_in,
    w_local, w_x_send, w_x_recv, w_dp_send, w_dp_recv, w_core_send, w_core_recv,
    ag_send, ag_recv, rs_send, rs_recv, quad_send, quad_recv,
    core_send, core_recv, dp_send, dp_recv, x_send, x_recv, full_send, full_recv,
    out_send, out_recv, lane_send, lane_recv, cv_send, cv_recv, xv_send, xv_recv,
    yv_send, yv_recv,
):
    section = lax.axis_index("section")
    group = lax.axis_index("dp")
    tensor = lax.axis_index("tensor")
    core = lax.rem(tensor, 2)
    lane = lax.rem(tensor // 2, LANE)
    high = tensor // (2 * LANE)
    own_pair = lane // 2
    other = 1 - core
    quad = high * 2 + core
    along_x = section * 2 + high

    def place(high_at, lane_at, core_at):
        return (high_at * LANE + lane_at) * 2 + core_at

    def to_lane(index):
        return {"tensor": place(high, index, core)}

    def to_quad(index):
        return {"tensor": place(index // 2, lane, lax.rem(index, 2))}

    def to_x(section_at, high_at):
        return {"section": section_at, "tensor": place(high_at, lane, core)}

    def to_dp(index):
        return {"dp": index}

    to_core = {"tensor": place(high, lane, other)}

    def next_of(own, step, count):
        return lax.rem(own + step, count)

    def remote(src, dst, send_sem, recv_sem, device):
        return pltpu.make_async_remote_copy(
            src_ref=src, dst_ref=dst, send_sem=send_sem, recv_sem=recv_sem,
            device_id=device, device_id_type=MESH,
        )

    def arrival(block, recv_sem):
        return remote(block, block, cv_send.at[0], recv_sem, to_core)

    sources = (small_in, attn_in, mlp_in)
    stores = (small_w, attn_w, mlp_w)

    def local_piece(kind):
        return pltpu.make_async_copy(
            sources[kind], stores[kind].at[section, quad], w_local.at[kind])

    for kind in range(3):
        local_piece(kind).start()

    barrier = pltpu.get_barrier_semaphore()
    friends = [to_lane(next_of(lane, step, LANE)) for step in range(1, LANE)]
    friends += [to_quad(next_of(quad, step, QUAD)) for step in range(1, QUAD)]
    friends += [to_x(1 - section, high), to_x(1 - section, 1 - high)]
    friends += [to_dp(next_of(group, step, DP)) for step in range(1, DP)]
    for friend in friends:
        pl.semaphore_signal(barrier, inc=1, device_id=friend, device_id_type=MESH)
    pl.semaphore_wait(barrier, len(friends))

    def is_own(layer, source):
        return jnp.logical_and(layer == section, source == high)

    def quarter(index):
        return pl.ds(pl.multiple_of(index * 128, 128), 128)

    def x_piece(kind, step):
        peer = next_of(along_x, step, 4)
        origin, there = sources[kind], stores[kind].at[section, quad]
        if kind == MLP:
            origin, there = origin.at[quarter(group)], there.at[quarter(group)]
        return remote(origin, there, w_x_send.at[kind, step], w_x_recv.at[kind, along_x],
                      to_x(peer // 2, lax.rem(peer, 2)))

    def dp_piece(layer, source, step):
        block = mlp_w.at[layer, source * 2 + core, quarter(group)]
        return remote(block, block, w_dp_send.at[layer * 2 + source, step],
                      w_dp_recv.at[layer * 2 + source, group], to_dp(next_of(group, step, DP)))

    def core_piece(kind, layer, source):
        block = stores[kind].at[layer, source * 2 + core]
        return remote(block, block, w_core_send.at[kind, layer * 2 + source],
                      w_core_recv.at[kind, layer * 2 + source], to_core)

    def send_pieces(kind):
        for step in range(1, 4):
            x_piece(kind, step).start()

    def spread_pieces(layer):
        for source in range(2):
            @pl.when(jnp.logical_not(is_own(layer, source)))
            def _():
                arrival(mlp_w.at[layer, source * 2 + core, quarter(group)],
                        w_x_recv.at[MLP, layer * 2 + source]).wait_recv()
                for step in range(1, DP):
                    dp_piece(layer, source, step).start()

    def relay_pieces(kind, layer):
        for source in range(2):
            @pl.when(is_own(layer, source))
            def _():
                local_piece(kind).wait()

            @pl.when(jnp.logical_not(is_own(layer, source)))
            def _():
                if kind == MLP:
                    for step in range(1, DP):
                        sender = next_of(group, step, DP)
                        arrival(mlp_w.at[layer, source * 2 + core, quarter(sender)],
                                w_dp_recv.at[layer * 2 + source, sender]).wait_recv()
                else:
                    arrival(stores[kind].at[layer, source * 2 + core],
                            w_x_recv.at[kind, layer * 2 + source]).wait_recv()

            core_piece(kind, layer, source).start()

    def take_pieces(kind, layer):
        for source in range(2):
            arrival(stores[kind].at[layer, source * 2 + other],
                    w_core_recv.at[kind, layer * 2 + source]).wait_recv()

    def gather_copy(layer, which, step):
        block = gathered.at[layer, which, lane]
        dest = jnp.bitwise_xor(lane, step)
        return remote(block, block, ag_send.at[step], ag_recv.at[which, lane], to_lane(dest))

    def gather_start(layer, which, rows):
        gathered[layer, which, lane] = rows
        for step in (2, 3, 1):
            gather_copy(layer, which, step).start()

    def gather_finish(layer, which):
        for step in (2, 3, 1):
            gather_copy(layer, which, step).wait_send()

    def gather_take(layer, which, pair):
        for side in range(2):
            source = pair * 2 + side

            @pl.when(source != lane)
            def _():
                arrival(gathered.at[layer, which, source], ag_recv.at[which, source]).wait_recv()

        return gathered[layer, which, pl.ds(pair * 2, 2)].reshape(2 * ROWS, D)

    def whole(layer, which):
        return gathered[layer, which].reshape(TOKENS, D)

    def part_copy(which, dest):
        return remote(parts.at[which % 2, dest], landed.at[which % 2, lane],
                      rs_send.at[dest], rs_recv.at[which, lane], to_lane(dest))

    def part_start(which, pair, rows):
        parts[which % 2, pl.ds(pair * 2, 2)] = rows.astype(BF16).reshape(2, ROWS, D)
        for side in range(2):
            dest = pair * 2 + side

            @pl.when(dest != lane)
            def _():
                part_copy(which, dest).start()

    def part_sum(which):
        total = parts[which % 2, lane].astype(F32)
        for step in range(1, LANE):
            source = next_of(lane, step, LANE)
            arrival(landed.at[which % 2, source], rs_recv.at[which, source]).wait_recv()
            total = total + landed[which % 2, source].astype(F32)
        for step in range(1, LANE):
            part_copy(which, next_of(lane, step, LANE)).wait_send()
        return total

    def each_pair(work, first=0):
        @pl.loop(0, PAIRS)
        def _(step):
            work(lax.rem(own_pair + first + step, PAIRS))

    def pair_rows(pair):
        return pl.ds(pl.multiple_of(pair * 2 * ROWS, 2 * ROWS), 2 * ROWS)

    d_att_out, d_mix_out, d_mix_got = att_out, qkv_out, qkv_got
    exchanges = ((qkv_out, qkv_got), (att_out, att_got), (d_att_out, d_att_got),
                 (d_mix_out, d_mix_got))

    def quad_copy(which, dest):
        origin, there = exchanges[which]
        return remote(origin.at[dest], there.at[quad], quad_send.at[which, dest],
                      quad_recv.at[which, quad], to_quad(dest))

    def quad_start(which):
        origin, there = exchanges[which]
        for step in (2, 3, 1):
            quad_copy(which, jnp.bitwise_xor(quad, step)).start()
        there[quad] = origin[quad]

    def quad_take(which):
        there = exchanges[which][1]
        for step in (1, 2, 3):
            source = jnp.bitwise_xor(quad, step)
            arrival(there.at[source], quad_recv.at[which, source]).wait_recv()

    def quad_finish(which):
        for step in (1, 2, 3):
            quad_copy(which, jnp.bitwise_xor(quad, step)).wait_send()

    def token_rows(source, half=0, length=TOKENS):
        return pl.ds(pl.multiple_of(source * TOKENS + half * length, length), length)

    def vector(layer, row):
        return small_w[layer, quad, row:row + 1]

    def all_biases(layer, first):
        row = slice(BIAS_ROW, BIAS_ROW + 1)
        return jnp.concatenate(
            [small_w[layer, member, row, first:first + 256] for member in range(QUAD)], axis=-1)

    def keep_inv(layer, which, inv):
        invs[layer, which] = jnp.broadcast_to(inv, (ROWS, 128))

    def get_inv(layer, which):
        return invs[layer, which, :, 0:1]

    def attn_weights(layer):
        return attn_w[layer].reshape(QUAD * 256, D)

    def out_weights(layer):
        return attn_w[layer, :, 192:256].reshape(QUAD * 64, D)

    def up_weights(layer):
        return mlp_w[layer, :, 0:256].reshape(QUAD * 256, D)

    def down_weights(layer):
        return mlp_w[layer, :, 256:512].reshape(QUAD * 256, D)

    send_pieces(SMALL)

    @pl.when(section == 0)
    def _():
        send_pieces(ATTN)
        send_pieces(MLP)

    xs[0] = x_in[...].astype(F32)
    vec[...] = jnp.zeros_like(vec)
    for layer in range(2):
        relay_pieces(SMALL, layer)

    @pl.loop(0, 2)
    def _(layer):
        unit, inv = normalize(xs[layer])
        units[layer, 0] = unit
        keep_inv(layer, 0, inv)
        gather_start(layer, 0, (unit * vector(layer, 0) + vector(layer, 1)).astype(BF16))

        @pl.when(layer == 0)
        def _():
            relay_pieces(ATTN, 0)
            for either in range(2):
                take_pieces(SMALL, either)

        take_pieces(ATTN, layer)
        qkv_bias = all_biases(layer, 0)

        def project(pair):
            rows = gather_take(layer, 0, pair)
            mixed = (dot_nt(rows, attn_weights(layer)) + qkv_bias).astype(BF16)
            for member in range(QUAD):
                qkv_out[member, pair_rows(pair)] = mixed[:, member * 256:member * 256 + 256]

        each_pair(project)
        quad_start(0)

        @pl.when(layer == 0)
        def _():
            @pl.when(section == 1)
            def _():
                send_pieces(ATTN)
                send_pieces(MLP)

            spread_pieces(0)

        @pl.when(layer == 1)
        def _():
            relay_pieces(MLP, 1)

        quad_take(0)
        for source in range(QUAD):
            block = qkv_got[source]
            queries[layer, token_rows(source)] = (block[:, 0:64].astype(F32) * 0.125).astype(BF16)
            keys[layer, token_rows(source)] = block[:, 64:128]
            values[layer, token_rows(source)] = block[:, 128:192]

        @pl.loop(0, QUAD)
        def _(step):
            source = lax.rem(quad + 1 + step, QUAD)
            for half in range(2):
                rows = token_rows(source, half, 128)
                scores = dot_nt(queries[layer, rows], keys[layer])
                grown = jnp.exp(scores - jnp.max(scores, axis=-1, keepdims=True))
                share = (grown / jnp.sum(grown, axis=-1, keepdims=True)).astype(BF16)
                probs[layer, rows] = share
                att_out[source, half * 128:half * 128 + 128] = dot_nn(
                    share, values[layer]).astype(BF16)

            @pl.when(source != quad)
            def _():
                quad_copy(1, source).start()

        att_got[quad] = att_out[quad]
        quad_take(1)
        attended[layer] = jnp.concatenate([att_got[member] for member in range(QUAD)], axis=-1)

        def project_out(pair):
            part_start(0, pair, dot_nn(attended[layer, pair_rows(pair)], out_weights(layer)))

        each_pair(project_out, 1)
        quad_finish(0)
        quad_finish(1)
        gather_finish(layer, 0)
        branch = part_sum(0) + vector(layer, 2)
        branches[layer, 0] = branch
        state = xs[layer] + vector(layer, 3) * branch
        hidden[...] = state

        unit, inv = normalize(state)
        units[layer, 1] = unit
        keep_inv(layer, 1, inv)
        gather_start(layer, 1, (unit * vector(layer, 4) + vector(layer, 5)).astype(BF16))

        @pl.when(layer == 0)
        def _():
            relay_pieces(MLP, 0)
            spread_pieces(1)

        take_pieces(MLP, layer)
        up_bias = all_biases(layer, 256)

        def feed(pair):
            rows = gather_take(layer, 1, pair)
            pre = dot_nt(rows, up_weights(layer)) + up_bias
            cdf = 0.5 + 0.5 * lax.erf(pre * 0.7071067811865476)
            bell = jnp.exp(-0.5 * pre * pre) * 0.3989422804014327
            value = (pre * cdf).astype(BF16)
            act[layer, pair_rows(pair)] = value
            slope[layer, pair_rows(pair)] = (cdf + pre * bell).astype(BF16)
            part_start(1, pair, dot_nn(value, down_weights(layer)))

        each_pair(feed)

        @pl.when(layer == 0)
        def _():
            relay_pieces(ATTN, 1)

        gather_finish(layer, 1)
        branch = part_sum(1) + vector(layer, 6)
        branches[layer, 1] = branch
        rounded = (hidden[...] + vector(layer, 7) * branch).astype(BF16)
        outs[0, layer] = rounded

        @pl.when(layer == 0)
        def _():
            xs[1] = rounded.astype(F32)

    def out_copy(which):
        return remote(outs.at[which, 1 - section], outs_in.at[which],
                      out_send.at[which], out_recv.at[which], to_x(1 - section, high))

    out_copy(0).start()

    grads = (grad_m, grad_a)
    from_core = (core_m, core_a)
    from_dp = (dp_m, dp_a)
    quarters = (part_m, part_a)
    from_x = (recv_m, recv_a)
    fulls = (full_m, full_a)
    lengths = (128, 64)

    def core_copy(kind):
        return remote(grads[kind].at[:, other], from_core[kind],
                      core_send.at[kind], core_recv.at[kind], to_core)

    def dp_rows(kind, index):
        length = lengths[kind]
        return pl.ds(pl.multiple_of(index * length, length), length)

    def dp_copy(kind, layer, step):
        dest = next_of(group, step, DP)
        return remote(grads[kind].at[:, core, dp_rows(kind, dest)],
                      from_dp[kind].at[layer, step - 1],
                      dp_send.at[kind, step], dp_recv.at[kind, layer, step], to_dp(dest))

    def x_copy(kind, layer, source):
        return remote(quarters[kind].at[layer, source], from_x[kind].at[along_x],
                      x_send.at[kind, layer * 2 + source], x_recv.at[kind, along_x],
                      to_x(layer, source))

    def core_done(kind, layer):
        core_copy(kind).wait()
        for source in range(2):
            grads[kind][source, core] = (
                grads[kind][source, core].astype(F32) + from_core[kind][source].astype(F32)
            ).astype(BF16)
        for step in range(1, DP):
            dp_copy(kind, layer, step).start()

    def dp_done(kind, layer):
        total = grads[kind][:, core, dp_rows(kind, group)].astype(F32)
        for step in range(1, DP):
            arrival(from_dp[kind].at[layer, step - 1],
                    dp_recv.at[kind, layer, step]).wait_recv()
            total = total + from_dp[kind][layer, step - 1].astype(F32)
        quarters[kind][layer] = total.astype(BF16)
        for source in range(2):
            @pl.when(jnp.logical_not(is_own(layer, source)))
            def _():
                x_copy(kind, layer, source).start()
        for step in range(1, DP):
            dp_copy(kind, layer, step).wait_send()

    def full_copy(kind, step):
        ref = fulls[kind]
        return remote(ref.at[group], ref.at[group], full_send.at[kind, step],
                      full_recv.at[kind, group], to_dp(next_of(group, step, DP)))

    def x_done(kind):
        total = quarters[kind][section, high].astype(F32)
        for step in range(1, 4):
            source = next_of(along_x, step, 4)
            arrival(from_x[kind].at[source], x_recv.at[kind, source]).wait_recv()
            total = total + from_x[kind][source].astype(F32)
        fulls[kind][group] = total.astype(BF16)
        for step in range(1, DP):
            full_copy(kind, step).start()

    cot[...] = cot_in[...]

    @pl.loop(0, 2)
    def _(turn):
        layer = 1 - turn
        above = cot[...]
        d_branch2 = (above * vector(layer, 7)).astype(BF16)
        gather_start(layer, 2, d_branch2)
        vec[layer, 7:8] = sum_rows(above * branches[layer, 1])
        vec[layer, 6:7] = sum_rows(d_branch2.astype(F32))

        @pl.when(turn == 1)
        def _():
            core_done(1, 1)

        def feed_back(pair):
            rows = gather_take(layer, 2, pair)
            d_act = dot_nt(rows, down_weights(layer))
            back = (d_act * slope[layer, pair_rows(pair)].astype(F32)).astype(BF16)
            d_pre[pair_rows(pair)] = back
            vec[layer, 8:9] += sum_rows(back.astype(F32))
            part_start(2, pair, dot_nn(back, up_weights(layer)))

        each_pair(feed_back)
        gather_finish(layer, 2)
        for member in range(QUAD):
            units_of = slice(member * 256, member * 256 + 256)
            at = (member // 2, member % 2)
            grad_m[at[0], at[1], 0:256] = dot_tn(d_pre[:, units_of], whole(layer, 1)).astype(BF16)
            grad_m[at[0], at[1], 256:512] = dot_tn(
                act[layer, :, units_of], whole(layer, 2)).astype(BF16)
        core_copy(0).start()
        d_normed = part_sum(2)
        unit, inv = units[layer, 1], get_inv(layer, 1)
        vec[layer, 4:5] = sum_rows(d_normed * unit)
        vec[layer, 5:6] = sum_rows(d_normed)
        d_hidden = above + normalize_back(d_normed, unit, inv, vector(layer, 4))
        hidden[...] = d_hidden
        d_branch = (d_hidden * vector(layer, 3)).astype(BF16)
        gather_start(layer, 3, d_branch)
        vec[layer, 3:4] = sum_rows(d_hidden * branches[layer, 0])
        vec[layer, 2:3] = sum_rows(d_branch.astype(F32))
        core_done(0, layer)

        def out_back(pair):
            rows = gather_take(layer, 3, pair)
            d_out = dot_nt(rows, out_weights(layer)).astype(BF16)
            for member in range(QUAD):
                d_att_out[member, pair_rows(pair)] = d_out[:, member * 64:member * 64 + 64]

        each_pair(out_back)
        quad_start(2)
        gather_finish(layer, 3)

        @pl.when(turn == 1)
        def _():
            dp_done(1, 1)

        out_grads = dot_tn(attended[layer], whole(layer, 3)).astype(BF16)
        d_keys[...] = jnp.zeros_like(d_keys)
        d_values[...] = jnp.zeros_like(d_values)
        quad_take(2)

        @pl.loop(0, QUAD)
        def _(source):
            score_grads = []
            for half in range(2):
                rows = token_rows(source, half, 128)
                d_share = dot_nt(d_att_got[source, half * 128:half * 128 + 128], values[layer])
                wide = probs[layer, rows].astype(F32)
                product = wide * d_share
                d_score = (product - wide * jnp.sum(product, axis=-1, keepdims=True)).astype(BF16)
                score_grads.append(d_score)
                d_mix_out[source, half * 128:half * 128 + 128, 0:64] = (
                    dot_nn(d_score, keys[layer]) * 0.125).astype(BF16)
            d_keys[...] += dot_tn(jnp.concatenate(score_grads, 0),
                                  queries[layer, token_rows(source)])
            d_values[...] += dot_tn(probs[layer, token_rows(source)], d_att_got[source])

        for source in range(QUAD):
            d_mix_out[source, :, 64:128] = d_keys[token_rows(source)].astype(BF16)
            d_mix_out[source, :, 128:192] = d_values[token_rows(source)].astype(BF16)
            d_mix_out[source, :, 192:256] = jnp.zeros((TOKENS, 64), BF16)
        quad_start(3)
        for member in range(QUAD):
            grad_a[member // 2, member % 2, 192:256] = out_grads[member * 64:member * 64 + 64]
        quad_take(3)

        def project_back(pair):
            rows = jnp.concatenate(
                [d_mix_got[member, pair_rows(pair)] for member in range(QUAD)], axis=-1)
            vec[layer, 9:10] += sum_rows(rows.astype(F32))
            part_start(3, pair, dot_nn(rows, attn_weights(layer)))

        each_pair(project_back, 1)
        for member in range(QUAD):
            grad_a[member // 2, member % 2, 0:192] = dot_tn(
                d_mix_got[member], whole(layer, 0))[0:192].astype(BF16)
        core_copy(1).start()
        quad_finish(2)
        quad_finish(3)
        dp_done(0, layer)
        d_normed = part_sum(3)
        unit, inv = units[layer, 0], get_inv(layer, 0)
        vec[layer, 0:1] = sum_rows(d_normed * unit)
        vec[layer, 1:2] = sum_rows(d_normed)
        rounded = (hidden[...] + normalize_back(d_normed, unit, inv, vector(layer, 0))).astype(BF16)
        outs[1, layer] = rounded
        cot[...] = rounded.astype(F32)

    core_done(1, 0)
    out_copy(1).start()
    x_done(0)

    def lane_copy(dest):
        return remote(vec.at[:, pl.ds(0, 8)], lane_vec.at[lane],
                      lane_send.at[dest], lane_recv.at[lane], to_lane(dest))

    for step in range(1, LANE):
        lane_copy(next_of(lane, step, LANE)).start()
    for step in range(1, LANE):
        source = next_of(lane, step, LANE)
        arrival(lane_vec.at[source], lane_recv.at[source]).wait_recv()
    for step in range(1, LANE):
        lane_copy(next_of(lane, step, LANE)).wait_send()
    for step in range(1, LANE):
        vec[:, 0:8] += lane_vec[next_of(lane, step, LANE)]
    cv_copy = remote(vec, core_vec, cv_send.at[0], cv_recv.at[0], to_core)
    cv_copy.start()
    cv_copy.wait()
    vec[...] += core_vec[...]

    def xv_copy(layer, source):
        return remote(vec.at[layer], x_vec.at[along_x], xv_send.at[layer * 2 + source],
                      xv_recv.at[along_x], to_x(layer, source))

    for layer in range(2):
        for source in range(2):
            @pl.when(jnp.logical_not(is_own(layer, source)))
            def _():
                xv_copy(layer, source).start()

    dp_done(1, 0)

    total = vec[section]
    for step in range(1, 4):
        source = next_of(along_x, step, 4)
        arrival(x_vec.at[source], xv_recv.at[source]).wait_recv()
        total = total + x_vec[source]
    dp_vec[group] = total

    def yv_copy(step):
        return remote(dp_vec.at[group], dp_vec.at[group], yv_send.at[step],
                      yv_recv.at[group], to_dp(next_of(group, step, DP)))

    for step in range(1, DP):
        yv_copy(step).start()
    x_done(1)

    for which, ref in ((0, so_ref), (1, ig_ref)):
        out_copy(which).wait()
        ref[section] = outs[which, section]
        ref[1 - section] = outs_in[which]

    for step in range(1, DP):
        source = next_of(group, step, DP)
        arrival(dp_vec.at[source], yv_recv.at[source]).wait_recv()
        total = total + dp_vec[source]
    sm_ref[...] = total

    for kind, ref in ((0, gm_ref), (1, ga_ref)):
        for step in range(1, DP):
            source = next_of(group, step, DP)
            arrival(fulls[kind].at[source], full_recv.at[kind, source]).wait_recv()
        ref[...] = fulls[kind][...].reshape(DP * lengths[kind], D)

    for kind in range(3):
        for step in range(1, 4):
            x_piece(kind, step).wait_send()
        for layer in range(2):
            for source in range(2):
                core_piece(kind, layer, source).wait_send()
    for layer in range(2):
        for source in range(2):
            @pl.when(jnp.logical_not(is_own(layer, source)))
            def _():
                for step in range(1, DP):
                    dp_piece(layer, source, step).wait_send()
                for kind in range(2):
                    x_copy(kind, layer, source).wait_send()
                xv_copy(layer, source).wait_send()
    for step in range(1, DP):
        yv_copy(step).wait_send()
        for kind in range(2):
            full_copy(kind, step).wait_send()


def run_layers(x_rows, cot_rows, small, attn, mlp):
    vmem = pl.BlockSpec(memory_space=pltpu.VMEM)
    anywhere = pl.BlockSpec(memory_space=pl.ANY)
    dma = pltpu.SemaphoreType.DMA
    every = QUAD * TOKENS
    scratch = [
        pltpu.VMEM((2, QUAD, 16, D), F32),
        pltpu.VMEM((2, QUAD, 256, D), BF16),
        pltpu.VMEM((2, QUAD, 512, D), BF16),
        pltpu.VMEM((2, GATHERS, LANE, ROWS, D), BF16),
        pltpu.VMEM((2, LANE, ROWS, D), BF16),
        pltpu.VMEM((2, LANE, ROWS, D), BF16),
        pltpu.VMEM((2, ROWS, D), F32),
        pltpu.VMEM((2, 2, ROWS, D), F32),
        pltpu.VMEM((2, 2, ROWS, 128), F32),
        pltpu.VMEM((2, 2, ROWS, D), F32),
        pltpu.VMEM((ROWS, D), F32),
        pltpu.VMEM((ROWS, D), F32),
        pltpu.VMEM((QUAD, TOKENS, 256), BF16),
        pltpu.VMEM((QUAD, TOKENS, 256), BF16),
        pltpu.VMEM((2, every, 64), BF16),
        pltpu.VMEM((2, every, 64), BF16),
        pltpu.VMEM((2, every, 64), BF16),
        pltpu.VMEM((QUAD, TOKENS, 64), BF16),
        pltpu.VMEM((QUAD, TOKENS, 64), BF16),
        pltpu.VMEM((2, TOKENS, 256), BF16),
        pltpu.VMEM((2, every, every), BF16),
        pltpu.VMEM((2, TOKENS, 1024), BF16),
        pltpu.VMEM((2, TOKENS, 1024), BF16),
        pltpu.VMEM((TOKENS, 1024), BF16),
        pltpu.VMEM((QUAD, TOKENS, 64), BF16),
        pltpu.VMEM((every, 64), F32),
        pltpu.VMEM((every, 64), F32),
        pltpu.VMEM((2, 2, 512, D), BF16),
        pltpu.VMEM((2, 2, 256, D), BF16),
        pltpu.VMEM((2, 512, D), BF16),
        pltpu.VMEM((2, 256, D), BF16),
        pltpu.VMEM((2, DP - 1, 2, 128, D), BF16),
        pltpu.VMEM((2, DP - 1, 2, 64, D), BF16),
        pltpu.VMEM((2, 2, 128, D), BF16),
        pltpu.VMEM((2, 2, 64, D), BF16),
        pltpu.VMEM((4, 128, D), BF16),
        pltpu.VMEM((4, 64, D), BF16),
        pltpu.VMEM((DP, 128, D), BF16),
        pltpu.VMEM((DP, 64, D), BF16),
        pltpu.VMEM((2, 16, D), F32),
        pltpu.VMEM((LANE, 2, 8, D), F32),
        pltpu.VMEM((2, 16, D), F32),
        pltpu.VMEM((4, 16, D), F32),
        pltpu.VMEM((DP, 16, D), F32),
        pltpu.VMEM((2, 2, ROWS, D), BF16),
        pltpu.VMEM((2, ROWS, D), BF16),
        dma((3,)), dma((3, 4)), dma((3, 4)),
        dma((4, DP)), dma((4, DP)), dma((3, 4)), dma((3, 4)),
        dma((LANE,)), dma((GATHERS, LANE)),
        dma((LANE,)), dma((GATHERS, LANE)),
        dma((4, QUAD)), dma((4, QUAD)),
        dma((2,)), dma((2,)),
        dma((2, DP)), dma((2, 2, DP)),
        dma((2, 4)), dma((2, 4)),
        dma((2, DP)), dma((2, DP)),
        dma((2,)), dma((2,)),
        dma((LANE,)), dma((LANE,)),
        dma((1,)), dma((1,)),
        dma((4,)), dma((4,)),
        dma((DP,)), dma((DP,)),
    ]
    return pl.pallas_call(
        kernel,
        out_shape=(
            jax.ShapeDtypeStruct((2, ROWS, D), BF16),
            jax.ShapeDtypeStruct((2, ROWS, D), BF16),
            jax.ShapeDtypeStruct((512, D), BF16),
            jax.ShapeDtypeStruct((256, D), BF16),
            jax.ShapeDtypeStruct((16, D), F32),
        ),
        in_specs=[vmem, vmem] + [anywhere] * 3,
        out_specs=(vmem,) * 5,
        scratch_shapes=scratch,
        name="two_layers",
        compiler_params=pltpu.CompilerParams(
            collective_id=0, has_side_effects=True, vmem_limit_bytes=63 * 2**20
        ),
    )(x_rows, cot_rows, small, attn, mlp)


def body(
    images, out_grad, live_images, attn_in, qv_bias, attn_out, mlp_in, mlp_bias, mlp_out, vectors
):
    section = lax.axis_index("section")
    tensor = lax.axis_index("tensor")
    quad = tensor // (2 * LANE) * 2 + lax.rem(tensor, 2)
    counts = live_images.reshape(-1, MICRO)
    totals = jnp.sum(counts, axis=0).astype(F32)
    own = lax.dynamic_slice(counts, (lax.axis_index("dp"), section), (1, 1))[0, 0]
    weight = jnp.where(own > 0, 1.0 / totals[section], F32(0.0))
    x_rows = lax.dynamic_index_in_dim(images, section, 0, keepdims=False)
    cot_rows = lax.dynamic_index_in_dim(out_grad, section, 0, keepdims=False).astype(F32) * weight
    gap = jnp.zeros((64,), F32)
    biases = jnp.concatenate(
        [qv_bias[0, 0], gap, qv_bias[0, 1], gap, mlp_bias[0], jnp.zeros((512,), F32)])
    small = jnp.concatenate([vectors[0], biases[None], jnp.zeros((7, D), F32)], axis=0)
    attn = jnp.concatenate([attn_in[0].transpose(1, 2, 0).reshape(192, D), attn_out[0]], axis=0)
    mlp = jnp.concatenate([mlp_in[0].T, mlp_out[0]], axis=0)
    section_out, section_in_grad, g_mlp, g_attn, sums = run_layers(
        x_rows, cot_rows, small, attn, mlp)
    g_mlp, g_attn = g_mlp.astype(F32), g_attn.astype(F32)
    g_up_bias = lax.dynamic_slice(sums, (8, quad * 256), (1, 256))
    g_qkv_bias = lax.dynamic_slice(sums, (9, quad * 256), (1, 256))
    return (
        section_out[None],
        section_in_grad[None],
        g_attn[0:192].reshape(3, 64, D).transpose(2, 0, 1)[None],
        jnp.concatenate([g_qkv_bias[:, 0:64], g_qkv_bias[:, 128:192]], axis=0)[None],
        g_attn[192:256][None],
        g_mlp[0:256].T[None],
        g_up_bias,
        g_mlp[256:512][None],
        sums[0:8][None],
    )


def solution(mesh):
    placed = (
        P("dp", "tensor", None),
        P("dp", "tensor", None),
        P(),
        P("section", None, None, "tensor"),
        P("section", None, "tensor"),
        P("section", "tensor", None),
        P("section", None, "tensor"),
        P("section", "tensor"),
        P("section", "tensor", None),
        P("section", None, None),
    )
    return jax.shard_map(
        body,
        mesh=mesh,
        in_specs=placed,
        out_specs=(
            P("section", "dp", "tensor", None),
            P("section", "dp", "tensor", None),
            P("section", None, None, "tensor"),
            P("section", None, "tensor"),
            P("section", "tensor", None),
            P("section", None, "tensor"),
            P("section", "tensor"),
            P("section", "tensor", None),
            P("section", None, None),
        ),
        check_vma=False,
    )
```

time: 409 us -> 321 us (0.78)
  Pallas kernels: 381 us -> 297 us
  local copies, waits for them, and re-layouts: 18.9 us -> 14.5 us
    pallas_call x1, Pallas kernels: 381 us -> 297 us  [run_layers(): pl.pallas_call(kernel, out_shape=(jax.ShapeDtypeStruct((2, ROWS, D), BF16...]
where the time goes in v2:
time: 321 us; the launch traced here: 320 us
  Pallas kernels  297 us (93%)
  local copies, waits for them, and re-layouts  14.5 us (5%)
  other arithmetic  7.13 us (2%)
    pallas_call x1, Pallas kernels, run_layers(): pl.pallas_call(kernel, out_shape=(jax.ShapeDtypeStruct((2, ROWS, D), BF16...  297 us

profile of v2, /device:TPU:6, one launch (start us, length us, event | category | flops | bytes accessed | tf_op | source)
XLA Modules:
  0.0 320.3 jit_solution(10649191462023061829)
XLA Ops:
  0.7 0.8 reshape.34
  1.5 0.6 dynamic_slice.21
  2.8 0.6 dynamic_slice.22
  4.1 1.6 multiply_bitcast_fusion.cot_in
  5.7 0.7 dynamic-slice_bitcast_fusion.x_in
  6.4 0.8 slice_bitcast_fusion.4
  7.2 0.8 concatenate.15
  8.0 1.5 maximum_maximum_fusion.small_in
  9.4 1.2 copy.21
  10.7 1.0 pad_maximum_fusion.mlp_in
  11.8 0.8 pad_maximum_fusion.1.attn_in
  12.6 296.6 %two_layers.1 = (bf16[2,64,1024]{2,1,0:T(8,128)(2,1)}, bf16[2,64,1024]{2,1,0:T(8,128)(2,1)}, bf16[512,1024]{1,0:T(8,128)(2,1)}, bf16[256,1024]{1,0:T(8,128)(2,1)}, f32[16,1024]{1,0:T(8,128)}) custom-call(bf16[64,1024]{1,0:T(8,128)(2,1)} %dynamic-slice_bitcast_fusion.x_in, f32[64,1024]{1,0:T(8,128)} %multiply_bitcast_fusion.cot_in, ...), custom_call_target="tpu_custom_call" | custom-call | tf_op jit(solution)/shard_map/two_layers/pallas_call | solution.py:767
  309.1 0.8 constant_dynamic-slice_fusion
  309.9 0.6 maximum_bitcast_fusion
  310.5 1.3 constant_dynamic-slice_fusion.2
  311.7 1.4 slice_bitcast_fusion.3
  313.1 1.5 convert_element_type.16
  314.6 1.2 slice_bitcast_fusion
  315.8 1.3 copy.22
  317.1 0.1 convert_element_type.15
  317.2 0.7 slice_bitcast_fusion.2
  317.9 1.0 slice.36
  318.9 0.7 copy.25
  319.6 0.7 copy.26
  (20 shorter events, 0.1 us)
Async XLA Ops:
  0.6 5.1 %copy-start = (bf16[2,64,1024]{2,1,0:T(8,128)(2,1)S(1)}, bf16[2,64,1024]{2,1,0:T(8,128)(2,1)}, u32[]{:S(2)}) copy-start(bf16[2,64,1024]{2,1,0:T(8,128)(2,1)} %param.10) | copy-start | bytes 786436
  0.7 10.0 %copy-start.2 = (bf16[1,256,1024]{2,1,0:T(8,128)(2,1)S(1)}, bf16[1,256,1024]{2,1,0:T(8,128)(2,1)}, u32[]{:S(2)}) copy-start(bf16[1,256,1024]{2,1,0:T(8,128)(2,1)} %param.18) | copy-start | bytes 1572868
  0.7 11.1 %copy-start.3 = (bf16[1,1024,3,64]{1,3,2,0:T(8,128)(2,1)S(1)}, bf16[1,1024,3,64]{1,3,2,0:T(8,128)(2,1)}, u32[]{:S(2)}) copy-start(bf16[1,1024,3,64]{1,3,2,0:T(8,128)(2,1)} %param.13) | copy-start | bytes 1179652
  0.7 11.1 %copy-start.6 = (bf16[1,64,1024]{2,1,0:T(8,128)(2,1)S(1)}, bf16[1,64,1024]{2,1,0:T(8,128)(2,1)}, u32[]{:S(2)}) copy-start(bf16[1,64,1024]{2,1,0:T(8,128)(2,1)} %param.15) | copy-start | bytes 393220
  315.8 1.3 copy-start.1
  317.1 1.8 copy-start.5
  317.1 2.5 copy-start.4

commit v3 on v2

--- a/solution.py
+++ b/solution.py
@@ -18,8 +18,10 @@
 TOKENS = LANE * ROWS
 DP = 4
 BIAS_ROW = 8
+XORS = (1, 3, 2, 0)
+OWN = 3
 GATHERS = 4
-SMALL, ATTN, MLP = range(3)
+SMALL, HEAD, REST, MLP = range(4)
 
 
 def dot_nn(a, b):
@@ -54,8 +56,8 @@
 
 
 def kernel(
-    x_in, cot_in, small_in, attn_in, mlp_in,
-    so_ref, ig_ref, gm_ref, ga_ref, sm_ref,
+    images, out_grad, live, qkv_in, out_in, up_in, down_in, qv_bias, up_bias_in, vectors_in,
+    so_ref, ig_ref, g_in_ref, g_out_ref, g_up_ref, g_down_ref, g_qv_ref, g_bias_ref, g_vec_ref,
     small_w, attn_w, mlp_w,
     gathered, parts, landed,
     xs, units, invs, branches, hidden, cot,
@@ -75,7 +77,6 @@
     core = lax.rem(tensor, 2)
     lane = lax.rem(tensor // 2, LANE)
     high = tensor // (2 * LANE)
-    own_pair = lane // 2
     other = 1 - core
     quad = high * 2 + core
     along_x = section * 2 + high
@@ -109,15 +110,23 @@
     def arrival(block, recv_sem):
         return remote(block, block, cv_send.at[0], recv_sem, to_core)
 
-    sources = (small_in, attn_in, mlp_in)
-    stores = (small_w, attn_w, mlp_w)
-
-    def local_piece(kind):
-        return pltpu.make_async_copy(
-            sources[kind], stores[kind].at[section, quad], w_local.at[kind])
-
-    for kind in range(3):
-        local_piece(kind).start()
+    own_attn = attn_w.at[section, quad]
+    own_mlp = mlp_w.at[section, quad]
+    landing = probs.at[1, :, pl.ds(0, 256)]
+    loads = [
+        pltpu.make_async_copy(origin, there, w_local.at[at]) for at, (origin, there) in enumerate((
+            (qkv_in, own_attn.at[pl.ds(0, 192)]),
+            (out_in, own_attn.at[pl.ds(192, 64)]),
+            (up_in, landing),
+            (down_in, own_mlp.at[pl.ds(256, 256)]),
+        ))
+    ]
+    for load in loads:
+        load.start()
+    small_w[section, quad, 0:8] = vectors_in[...]
+    gap = jnp.zeros((1, 64), F32)
+    small_w[section, quad, 8:9] = jnp.concatenate(
+        [qv_bias[0:1], gap, qv_bias[1:2], gap, up_bias_in[...], jnp.zeros((1, 512), F32)], axis=1)
 
     barrier = pltpu.get_barrier_semaphore()
     friends = [to_lane(next_of(lane, step, LANE)) for step in range(1, LANE)]
@@ -131,121 +140,129 @@
     def is_own(layer, source):
         return jnp.logical_and(layer == section, source == high)
 
-    def quarter(index):
-        return pl.ds(pl.multiple_of(index * 128, 128), 128)
-
-    def x_piece(kind, step):
+    def piece(kind, layer, member):
+        if kind == SMALL:
+            return small_w.at[layer, member]
+        if kind == MLP:
+            return mlp_w.at[layer, member]
+        return attn_w.at[layer, member, pl.ds((kind - HEAD) * 128, 128)]
+
+    def by_quarters(kind, layer):
+        return kind == MLP or (kind != SMALL and (layer == 1 or kind == HEAD))
+
+    def quarter(kind, layer, member, index):
+        if kind == MLP:
+            return mlp_w.at[layer, member, pl.ds(pl.multiple_of(index * 128, 128), 128)]
+        first = pl.multiple_of((kind - HEAD) * 128 + index * 32, 32)
+        return attn_w.at[layer, member, pl.ds(first, 32)]
+
+    def x_block(kind, layer, member):
+        if by_quarters(kind, layer):
+            return quarter(kind, layer, member, group)
+        return piece(kind, layer, member)
+
+    def x_piece(kind, layer, step):
         peer = next_of(along_x, step, 4)
-        origin, there = sources[kind], stores[kind].at[section, quad]
-        if kind == MLP:
-            origin, there = origin.at[quarter(group)], there.at[quarter(group)]
-        return remote(origin, there, w_x_send.at[kind, step], w_x_recv.at[kind, along_x],
+        block = x_block(kind, layer, quad)
+        return remote(block, block, w_x_send.at[kind, step], w_x_recv.at[kind, along_x],
                       to_x(peer // 2, lax.rem(peer, 2)))
 
-    def dp_piece(layer, source, step):
-        block = mlp_w.at[layer, source * 2 + core, quarter(group)]
-        return remote(block, block, w_dp_send.at[layer * 2 + source, step],
-                      w_dp_recv.at[layer * 2 + source, group], to_dp(next_of(group, step, DP)))
+    def dp_piece(kind, layer, source, step):
+        block = quarter(kind, layer, source * 2 + core, group)
+        return remote(block, block, w_dp_send.at[kind, layer * 2 + source, step],
+                      w_dp_recv.at[kind, layer * 2 + source, group],
+                      to_dp(next_of(group, step, DP)))
 
     def core_piece(kind, layer, source):
-        block = stores[kind].at[layer, source * 2 + core]
+        block = piece(kind, layer, source * 2 + core)
         return remote(block, block, w_core_send.at[kind, layer * 2 + source],
                       w_core_recv.at[kind, layer * 2 + source], to_core)
 
-    def send_pieces(kind):
-        for step in range(1, 4):
-            x_piece(kind, step).start()
-
-    def spread_pieces(layer):
+    def send_pieces(kind, layer):
+        @pl.when(section == layer)
+        def _():
+            for step in range(1, 4):
+                x_piece(kind, layer, step).start()
+
+    def spread_pieces(kind, layer):
         for source in range(2):
             @pl.when(jnp.logical_not(is_own(layer, source)))
             def _():
-                arrival(mlp_w.at[layer, source * 2 + core, quarter(group)],
-                        w_x_recv.at[MLP, layer * 2 + source]).wait_recv()
+                arrival(x_block(kind, layer, source * 2 + core),
+                        w_x_recv.at[kind, layer * 2 + source]).wait_recv()
                 for step in range(1, DP):
-                    dp_piece(layer, source, step).start()
+                    dp_piece(kind, layer, source, step).start()
 
     def relay_pieces(kind, layer):
         for source in range(2):
-            @pl.when(is_own(layer, source))
-            def _():
-                local_piece(kind).wait()
-
             @pl.when(jnp.logical_not(is_own(layer, source)))
             def _():
-                if kind == MLP:
+                if by_quarters(kind, layer):
                     for step in range(1, DP):
                         sender = next_of(group, step, DP)
-                        arrival(mlp_w.at[layer, source * 2 + core, quarter(sender)],
-                                w_dp_recv.at[layer * 2 + source, sender]).wait_recv()
+                        arrival(quarter(kind, layer, source * 2 + core, sender),
+                                w_dp_recv.at[kind, layer * 2 + source, sender]).wait_recv()
                 else:
-                    arrival(stores[kind].at[layer, source * 2 + core],
+                    arrival(x_block(kind, layer, source * 2 + core),
                             w_x_recv.at[kind, layer * 2 + source]).wait_recv()
 
             core_piece(kind, layer, source).start()
 
     def take_pieces(kind, layer):
         for source in range(2):
-            arrival(stores[kind].at[layer, source * 2 + other],
+            arrival(piece(kind, layer, source * 2 + other),
                     w_core_recv.at[kind, layer * 2 + source]).wait_recv()
 
-    def gather_copy(layer, which, step):
-        block = gathered.at[layer, which, lane]
-        dest = jnp.bitwise_xor(lane, step)
-        return remote(block, block, ag_send.at[step], ag_recv.at[which, lane], to_lane(dest))
+    def lane_of(slot):
+        return jnp.bitwise_xor(lane, XORS[slot])
+
+    def gather_copy(layer, which, slot):
+        return remote(gathered.at[layer, which, OWN], gathered.at[layer, which, slot],
+                      ag_send.at[slot], ag_recv.at[which, slot], to_lane(lane_of(slot)))
 
     def gather_start(layer, which, rows):
-        gathered[layer, which, lane] = rows
-        for step in (2, 3, 1):
-            gather_copy(layer, which, step).start()
+        gathered[layer, which, OWN] = rows
+        for slot in range(OWN):
+            gather_copy(layer, which, slot).start()
 
     def gather_finish(layer, which):
-        for step in (2, 3, 1):
-            gather_copy(layer, which, step).wait_send()
-
-    def gather_take(layer, which, pair):
-        for side in range(2):
-            source = pair * 2 + side
-
-            @pl.when(source != lane)
-            def _():
-                arrival(gathered.at[layer, which, source], ag_recv.at[which, source]).wait_recv()
-
-        return gathered[layer, which, pl.ds(pair * 2, 2)].reshape(2 * ROWS, D)
+        for slot in range(OWN):
+            gather_copy(layer, which, slot).wait_send()
+
+    def gather_take(layer, which, step):
+        for slot in (2 * step, 2 * step + 1):
+            if slot != OWN:
+                arrival(gathered.at[layer, which, slot], ag_recv.at[which, slot]).wait_recv()
+        return gathered[layer, which, 2 * step:2 * step + 2].reshape(2 * ROWS, D)
 
     def whole(layer, which):
         return gathered[layer, which].reshape(TOKENS, D)
 
-    def part_copy(which, dest):
-        return remote(parts.at[which % 2, dest], landed.at[which % 2, lane],
-                      rs_send.at[dest], rs_recv.at[which, lane], to_lane(dest))
-
-    def part_start(which, pair, rows):
-        parts[which % 2, pl.ds(pair * 2, 2)] = rows.astype(BF16).reshape(2, ROWS, D)
-        for side in range(2):
-            dest = pair * 2 + side
-
-            @pl.when(dest != lane)
-            def _():
-                part_copy(which, dest).start()
+    def part_copy(which, slot):
+        return remote(parts.at[which % 2, slot], landed.at[which % 2, slot],
+                      rs_send.at[slot], rs_recv.at[which, slot], to_lane(lane_of(slot)))
+
+    def part_start(which, step, rows):
+        parts[which % 2, 2 * step:2 * step + 2] = rows.astype(BF16).reshape(2, ROWS, D)
+        for slot in (2 * step, 2 * step + 1):
+            if slot != OWN:
+                part_copy(which, slot).start()
 
     def part_sum(which):
-        total = parts[which % 2, lane].astype(F32)
-        for step in range(1, LANE):
-            source = next_of(lane, step, LANE)
-            arrival(landed.at[which % 2, source], rs_recv.at[which, source]).wait_recv()
-            total = total + landed[which % 2, source].astype(F32)
-        for step in range(1, LANE):
-            part_copy(which, next_of(lane, step, LANE)).wait_send()
+        total = parts[which % 2, OWN].astype(F32)
+        for slot in range(OWN):
+            arrival(landed.at[which % 2, slot], rs_recv.at[which, slot]).wait_recv()
+            total = total + landed[which % 2, slot].astype(F32)
+        for slot in range(OWN):
+            part_copy(which, slot).wait_send()
         return total
 
-    def each_pair(work, first=0):
-        @pl.loop(0, PAIRS)
-        def _(step):
-            work(lax.rem(own_pair + first + step, PAIRS))
-
-    def pair_rows(pair):
-        return pl.ds(pl.multiple_of(pair * 2 * ROWS, 2 * ROWS), 2 * ROWS)
+    def each_pair(work):
+        for step in range(PAIRS):
+            work(step)
+
+    def pair_rows(step):
+        return slice(step * 2 * ROWS, (step + 1) * 2 * ROWS)
 
     d_att_out, d_mix_out, d_mix_got = att_out, qkv_out, qkv_got
     exchanges = ((qkv_out, qkv_got), (att_out, att_got), (d_att_out, d_att_got),
@@ -255,6 +272,10 @@
         origin, there = exchanges[which]
         return remote(origin.at[dest], there.at[quad], quad_send.at[which, dest],
                       quad_recv.at[which, quad], to_quad(dest))
+
+    def half_copy(half, dest):
+        return remote(qkv_out.at[dest, pair_rows(half)], qkv_got.at[quad, pair_rows(half)],
+                      quad_send.at[4 * half, dest], quad_recv.at[4 * half, quad], to_quad(dest))
 
     def quad_start(which):
         origin, there = exchanges[which]
@@ -301,14 +322,19 @@
     def down_weights(layer):
         return mlp_w[layer, :, 256:512].reshape(QUAD * 256, D)
 
-    send_pieces(SMALL)
-
-    @pl.when(section == 0)
-    def _():
-        send_pieces(ATTN)
-        send_pieces(MLP)
-
-    xs[0] = x_in[...].astype(F32)
+    for layer in range(2):
+        send_pieces(SMALL, layer)
+    loads[0].wait()
+    loads[1].wait()
+    send_pieces(HEAD, 0)
+    send_pieces(REST, 0)
+    loads[2].wait()
+    for part in range(4):
+        mlp_w[section, quad, 0:256, part * 256:part * 256 + 256] = (
+            probs[1, part * 256:part * 256 + 256, 0:256].astype(F32).T.astype(BF16))
+    loads[3].wait()
+    send_pieces(MLP, 0)
+    xs[0] = images[section].astype(F32)
     vec[...] = jnp.zeros_like(vec)
     for layer in range(2):
         relay_pieces(SMALL, layer)
@@ -322,11 +348,14 @@
 
         @pl.when(layer == 0)
         def _():
-            relay_pieces(ATTN, 0)
+            spread_pieces(HEAD, 0)
+            relay_pieces(REST, 0)
+            relay_pieces(HEAD, 0)
             for either in range(2):
                 take_pieces(SMALL, either)
 
-        take_pieces(ATTN, layer)
+        take_pieces(REST, layer)
+        take_pieces(HEAD, layer)
         qkv_bias = all_biases(layer, 0)
 
         def project(pair):
@@ -334,24 +363,27 @@
             mixed = (dot_nt(rows, attn_weights(layer)) + qkv_bias).astype(BF16)
             for member in range(QUAD):
                 qkv_out[member, pair_rows(pair)] = mixed[:, member * 256:member * 256 + 256]
+            for step in (2, 3, 1):
+                half_copy(pair, jnp.bitwise_xor(quad, step)).start()
 
         each_pair(project)
-        quad_start(0)
+        qkv_got[quad] = qkv_out[quad]
 
         @pl.when(layer == 0)
         def _():
-            @pl.when(section == 1)
-            def _():
-                send_pieces(ATTN)
-                send_pieces(MLP)
-
-            spread_pieces(0)
+            for kind in (HEAD, REST, MLP):
+                send_pieces(kind, 1)
+            spread_pieces(MLP, 0)
 
         @pl.when(layer == 1)
         def _():
             relay_pieces(MLP, 1)
 
-        quad_take(0)
+        for half in range(PAIRS):
+            for step in (1, 2, 3):
+                source = jnp.bitwise_xor(quad, step)
+                arrival(qkv_got.at[source, pair_rows(half)],
+                        quad_recv.at[4 * half, source]).wait_recv()
         for source in range(QUAD):
             block = qkv_got[source]
             queries[layer, token_rows(source)] = (block[:, 0:64].astype(F32) * 0.125).astype(BF16)
@@ -381,8 +413,10 @@
         def project_out(pair):
             part_start(0, pair, dot_nn(attended[layer, pair_rows(pair)], out_weights(layer)))
 
-        each_pair(project_out, 1)
-        quad_finish(0)
+        each_pair(project_out)
+        for half in range(PAIRS):
+            for step in (1, 2, 3):
+                half_copy(half, jnp.bitwise_xor(quad, step)).wait_send()
         quad_finish(1)
         gather_finish(layer, 0)
         branch = part_sum(0) + vector(layer, 2)
@@ -398,7 +432,8 @@
         @pl.when(layer == 0)
         def _():
             relay_pieces(MLP, 0)
-            spread_pieces(1)
+            for kind in (HEAD, REST, MLP):
+                spread_pieces(kind, 1)
 
         take_pieces(MLP, layer)
         up_bias = all_biases(layer, 256)
@@ -417,7 +452,8 @@
 
         @pl.when(layer == 0)
         def _():
-            relay_pieces(ATTN, 1)
+            relay_pieces(HEAD, 1)
+            relay_pieces(REST, 1)
 
         gather_finish(layer, 1)
         branch = part_sum(1) + vector(layer, 6)
@@ -500,7 +536,12 @@
         for step in range(1, DP):
             full_copy(kind, step).start()
 
-    cot[...] = cot_in[...]
+    mine = live[group * MICRO + section]
+    everyone = live[section]
+    for step in range(1, DP):
+        everyone = everyone + live[step * MICRO + section]
+    weight = jnp.where(mine > 0, 1.0 / jnp.full((1, D), everyone, jnp.int32).astype(F32), 0.0)
+    cot[...] = out_grad[section].astype(F32) * weight
 
     @pl.loop(0, 2)
     def _(turn):
@@ -594,7 +635,7 @@
             vec[layer, 9:10] += sum_rows(rows.astype(F32))
             part_start(3, pair, dot_nn(rows, attn_weights(layer)))
 
-        each_pair(project_back, 1)
+        each_pair(project_back)
         for member in range(QUAD):
             grad_a[member // 2, member % 2, 0:192] = dot_tn(
                 d_mix_got[member], whole(layer, 0))[0:192].astype(BF16)
@@ -668,36 +709,53 @@
         source = next_of(group, step, DP)
         arrival(dp_vec.at[source], yv_recv.at[source]).wait_recv()
         total = total + dp_vec[source]
-    sm_ref[...] = total
-
-    for kind, ref in ((0, gm_ref), (1, ga_ref)):
+    for step in range(1, DP):
+        yv_copy(step).wait_send()
+    g_vec_ref[...] = total[0:8]
+    dp_vec[group] = total
+    bias_of = dp_vec[group, :, pl.ds(pl.multiple_of(quad * 256, 256), 256)]
+    g_bias_ref[...] = bias_of[8:9]
+    g_qv_ref[...] = jnp.concatenate([bias_of[9:10, 0:64], bias_of[9:10, 128:192]], axis=0)
+
+    for kind in range(2):
         for step in range(1, DP):
             source = next_of(group, step, DP)
             arrival(fulls[kind].at[source], full_recv.at[kind, source]).wait_recv()
-        ref[...] = fulls[kind][...].reshape(DP * lengths[kind], D)
-
-    for kind in range(3):
-        for step in range(1, 4):
-            x_piece(kind, step).wait_send()
-        for layer in range(2):
-            for source in range(2):
+        if kind == 0:
+            for part in range(4):
+                g_up_ref[part * 256:part * 256 + 256] = full_m[
+                    0:2, :, part * 256:part * 256 + 256].reshape(256, 256).astype(F32).T.astype(BF16)
+            g_down_ref[...] = full_m[2:4].reshape(256, D)
+        else:
+            g_in_ref[...] = full_a[0:3].reshape(192, D)
+            g_out_ref[...] = full_a[3]
+
+    for layer in range(2):
+        @pl.when(section == layer)
+        def _():
+            for kind in range(4):
+                for step in range(1, 4):
+                    x_piece(kind, layer, step).wait_send()
+
+        for source in range(2):
+            for kind in range(4):
                 core_piece(kind, layer, source).wait_send()
-    for layer in range(2):
-        for source in range(2):
+
             @pl.when(jnp.logical_not(is_own(layer, source)))
             def _():
-                for step in range(1, DP):
-                    dp_piece(layer, source, step).wait_send()
+                for kind in (HEAD, REST, MLP):
+                    if by_quarters(kind, layer):
+                        for step in range(1, DP):
+                            dp_piece(kind, layer, source, step).wait_send()
                 for kind in range(2):
                     x_copy(kind, layer, source).wait_send()
                 xv_copy(layer, source).wait_send()
     for step in range(1, DP):
-        yv_copy(step).wait_send()
         for kind in range(2):
             full_copy(kind, step).wait_send()
 
 
-def run_layers(x_rows, cot_rows, small, attn, mlp):
+def run_layers(*operands):
     vmem = pl.BlockSpec(memory_space=pltpu.VMEM)
     anywhere = pl.BlockSpec(memory_space=pl.ANY)
     dma = pltpu.SemaphoreType.DMA
@@ -749,11 +807,11 @@
         pltpu.VMEM((DP, 16, D), F32),
         pltpu.VMEM((2, 2, ROWS, D), BF16),
         pltpu.VMEM((2, ROWS, D), BF16),
-        dma((3,)), dma((3, 4)), dma((3, 4)),
-        dma((4, DP)), dma((4, DP)), dma((3, 4)), dma((3, 4)),
+        dma((4,)), dma((4, 4)), dma((4, 4)),
+        dma((4, 4, DP)), dma((4, 4, DP)), dma((4, 4)), dma((4, 4)),
         dma((LANE,)), dma((GATHERS, LANE)),
         dma((LANE,)), dma((GATHERS, LANE)),
-        dma((4, QUAD)), dma((4, QUAD)),
+        dma((5, QUAD)), dma((5, QUAD)),
         dma((2,)), dma((2,)),
         dma((2, DP)), dma((2, 2, DP)),
         dma((2, 4)), dma((2, 4)),
@@ -769,53 +827,40 @@
         out_shape=(
             jax.ShapeDtypeStruct((2, ROWS, D), BF16),
             jax.ShapeDtypeStruct((2, ROWS, D), BF16),
-            jax.ShapeDtypeStruct((512, D), BF16),
+            jax.ShapeDtypeStruct((192, D), BF16),
+            jax.ShapeDtypeStruct((64, D), BF16),
+            jax.ShapeDtypeStruct((D, 256), BF16),
             jax.ShapeDtypeStruct((256, D), BF16),
-            jax.ShapeDtypeStruct((16, D), F32),
+            jax.ShapeDtypeStruct((2, 64), F32),
+            jax.ShapeDtypeStruct((1, 256), F32),
+            jax.ShapeDtypeStruct((8, D), F32),
         ),
-        in_specs=[vmem, vmem] + [anywhere] * 3,
-        out_specs=(vmem,) * 5,
+        in_specs=[vmem, vmem, pl.BlockSpec(memory_space=pltpu.SMEM)] + [anywhere] * 4 + [vmem] * 3,
+        out_specs=(vmem,) * 9,
         scratch_shapes=scratch,
         name="two_layers",
         compiler_params=pltpu.CompilerParams(
             collective_id=0, has_side_effects=True, vmem_limit_bytes=63 * 2**20
         ),
-    )(x_rows, cot_rows, small, attn, mlp)
+    )(*operands)
 
 
 def body(
     images, out_grad, live_images, attn_in, qv_bias, attn_out, mlp_in, mlp_bias, mlp_out, vectors
 ):
-    section = lax.axis_index("section")
-    tensor = lax.axis_index("tensor")
-    quad = tensor // (2 * LANE) * 2 + lax.rem(tensor, 2)
-    counts = live_images.reshape(-1, MICRO)
-    totals = jnp.sum(counts, axis=0).astype(F32)
-    own = lax.dynamic_slice(counts, (lax.axis_index("dp"), section), (1, 1))[0, 0]
-    weight = jnp.where(own > 0, 1.0 / totals[section], F32(0.0))
-    x_rows = lax.dynamic_index_in_dim(images, section, 0, keepdims=False)
-    cot_rows = lax.dynamic_index_in_dim(out_grad, section, 0, keepdims=False).astype(F32) * weight
-    gap = jnp.zeros((64,), F32)
-    biases = jnp.concatenate(
-        [qv_bias[0, 0], gap, qv_bias[0, 1], gap, mlp_bias[0], jnp.zeros((512,), F32)])
-    small = jnp.concatenate([vectors[0], biases[None], jnp.zeros((7, D), F32)], axis=0)
-    attn = jnp.concatenate([attn_in[0].transpose(1, 2, 0).reshape(192, D), attn_out[0]], axis=0)
-    mlp = jnp.concatenate([mlp_in[0].T, mlp_out[0]], axis=0)
-    section_out, section_in_grad, g_mlp, g_attn, sums = run_layers(
-        x_rows, cot_rows, small, attn, mlp)
-    g_mlp, g_attn = g_mlp.astype(F32), g_attn.astype(F32)
-    g_up_bias = lax.dynamic_slice(sums, (8, quad * 256), (1, 256))
-    g_qkv_bias = lax.dynamic_slice(sums, (9, quad * 256), (1, 256))
+    section_out, section_in_grad, g_in, g_out, g_up, g_down, g_qv, g_bias, g_vec = run_layers(
+        images, out_grad, live_images, attn_in[0].transpose(1, 2, 0).reshape(192, D),
+        attn_out[0], mlp_in[0], mlp_out[0], qv_bias[0], mlp_bias, vectors[0])
     return (
         section_out[None],
         section_in_grad[None],
-        g_attn[0:192].reshape(3, 64, D).transpose(2, 0, 1)[None],
-        jnp.concatenate([g_qkv_bias[:, 0:64], g_qkv_bias[:, 128:192]], axis=0)[None],
-        g_attn[192:256][None],
-        g_mlp[0:256].T[None],
-        g_up_bias,
-        g_mlp[256:512][None],
-        sums[0:8][None],
+        g_in.astype(F32).reshape(3, 64, D).transpose(2, 0, 1)[None],
+        g_qv[None],
+        g_out.astype(F32)[None],
+        g_up.astype(F32)[None],
+        g_bias,
+        g_down.astype(F32)[None],
+        g_vec[None],
     )
 
 

time: 321 us -> 272 us (0.85)
  Pallas kernels: 297 us -> 260 us
  local copies, waits for them, and re-layouts: 14.5 us -> 3.93 us
    pallas_call x1, Pallas kernels: 297 us -> 260 us  [run_layers(): pl.pallas_call(kernel, out_shape=(jax.ShapeDtypeStruct((2, ROWS, D), BF16...]
    broadcast_in_dim x1 -> x4, other arithmetic: 0.57 us -> 4.92 us  [the longest x1 2.18 us: body(): g_down.astype(F32)[None]]
    concatenate x3 -> x0, other arithmetic: 3.33 us -> none  [the longest x1 1.46 us: body(): jnp.concatenate([vectors[0], biases[None], jnp.zeros((7, D), F32)], axis=0)]
    broadcast_in_dim x6 -> x0, local copies, waits for them, and re-layouts: 3.27 us -> none  [the longest x1 1.37 us: body(): sums[0:8][None]]
where the time goes in v3:
time: 272 us; the launch traced here: 269 us
  Pallas kernels  260 us (96%)
  other arithmetic  4.92 us (2%)
  local copies, waits for them, and re-layouts  3.93 us (1%)
    pallas_call x1, Pallas kernels, run_layers(): pl.pallas_call(kernel, out_shape=(jax.ShapeDtypeStruct((2, ROWS, D), BF16...  260 us

profile of v3, /device:TPU:6, one launch (start us, length us, event | category | flops | bytes accessed | tf_op | source)
XLA Modules:
  0.0 269.4 jit_solution(12453874692567874672)
XLA Ops:
  0.6 259.9 %two_layers.1 = (bf16[2,64,1024]{2,1,0:T(8,128)(2,1)}, bf16[2,64,1024]{2,1,0:T(8,128)(2,1)}, bf16[192,1024]{1,0:T(8,128)(2,1)}, bf16[64,1024]{1,0:T(8,128)(2,1)}...) custom-call(bf16[2,64,1024]{2,1,0:T(8,128)(2,1)} %images.1, ...), custom_call_target="tpu_custom_call" | custom-call | tf_op jit(solution)/shard_map/two_layers/pallas_call | solution.py:825
  260.5 0.0 copy-start
  260.5 2.2 bitcast_convert_fusion
  262.7 0.0 copy-done
  262.7 0.0 copy-start.1
  262.7 1.0 bitcast_convert_fusion.1
  263.8 0.0 copy-done.1
  263.8 0.0 copy-start.4
  263.8 1.0 convert_bitcast_fusion
  264.7 0.0 copy-start.3
  264.7 0.0 copy-done.4
  264.7 0.7 bitcast_convert_fusion.2
  265.4 0.3 copy-done.3
  265.8 0.0 copy-start.2
  265.8 0.7 copy.24
  266.5 0.3 copy-done.2
  266.8 0.0 copy-start.7
  266.8 0.7 copy.25
  267.5 0.0 copy-done.7
  267.5 0.6 copy.26
  268.1 0.1 copy-done.6
  268.2 0.6 copy.27
  268.8 0.0 copy-done.5
  268.8 0.6 copy.28
  (2 shorter events, 0.0 us)
Async XLA Ops:
  260.5 2.2 copy-start
  262.7 1.1 copy-start.1
  263.8 1.0 copy-start.4
  264.7 1.0 copy-start.3
  265.8 1.0 copy-start.2
  266.8 0.7 copy-start.7
  266.8 1.9 copy-start.5
  267.5 0.7 copy-start.6

commit v4 on v3

--- a/solution.py
+++ b/solution.py
@@ -62,7 +62,7 @@
     gathered, parts, landed,
     xs, units, invs, branches, hidden, cot,
     qkv_out, qkv_got, queries, keys, values, att_out, att_got, attended, probs,
-    act, slope, d_pre, d_att_got, d_keys, d_values,
+    act, slope, d_pre, d_mixed, d_att_got, d_keys, d_values,
     grad_m, grad_a, core_m, core_a, dp_m, dp_a, part_m, part_a, recv_m, recv_a, full_m, full_a,
     vec, lane_vec, core_vec, x_vec, dp_vec, outs, outs_in,
     w_local, w_x_send, w_x_recv, w_dp_send, w_dp_recv, w_core_send, w_core_recv,
@@ -273,8 +273,19 @@
         return remote(origin.at[dest], there.at[quad], quad_send.at[which, dest],
                       quad_recv.at[which, quad], to_quad(dest))
 
+    def pack_rows(member, half, query_key, value):
+        qkv_out[member, half, 0:128] = query_key
+        qkv_out[member, half, 128:192] = jnp.concatenate([value[0:64], value[64:128]], axis=-1)
+
+    def unpack_values(source, half):
+        block = qkv_got[source, half, 128:192]
+        return jnp.concatenate([block[:, 0:64], block[:, 64:128]], axis=0)
+
+    def unpack_halves(block):
+        return jnp.concatenate([block[:, 0:64], block[:, 64:128]], axis=0)
+
     def half_copy(half, dest):
-        return remote(qkv_out.at[dest, pair_rows(half)], qkv_got.at[quad, pair_rows(half)],
+        return remote(qkv_out.at[dest, half], qkv_got.at[quad, half],
                       quad_send.at[4 * half, dest], quad_recv.at[4 * half, quad], to_quad(dest))
 
     def quad_start(which):
@@ -362,7 +373,9 @@
             rows = gather_take(layer, 0, pair)
             mixed = (dot_nt(rows, attn_weights(layer)) + qkv_bias).astype(BF16)
             for member in range(QUAD):
-                qkv_out[member, pair_rows(pair)] = mixed[:, member * 256:member * 256 + 256]
+                first = member * 256
+                pack_rows(member, pair, mixed[:, first:first + 128],
+                          mixed[:, first + 128:first + 192])
             for step in (2, 3, 1):
                 half_copy(pair, jnp.bitwise_xor(quad, step)).start()
 
@@ -382,25 +395,28 @@
         for half in range(PAIRS):
             for step in (1, 2, 3):
                 source = jnp.bitwise_xor(quad, step)
-                arrival(qkv_got.at[source, pair_rows(half)],
+                arrival(qkv_got.at[source, half],
                         quad_recv.at[4 * half, source]).wait_recv()
         for source in range(QUAD):
-            block = qkv_got[source]
-            queries[layer, token_rows(source)] = (block[:, 0:64].astype(F32) * 0.125).astype(BF16)
-            keys[layer, token_rows(source)] = block[:, 64:128]
-            values[layer, token_rows(source)] = block[:, 128:192]
+            for half in range(PAIRS):
+                rows = token_rows(source, half, 128)
+                block = qkv_got[source, half, 0:128]
+                queries[layer, rows] = (block[:, 0:64].astype(F32) * 0.125).astype(BF16)
+                keys[layer, rows] = block[:, 64:128]
+                values[layer, rows] = unpack_values(source, half)
 
         @pl.loop(0, QUAD)
         def _(step):
             source = lax.rem(quad + 1 + step, QUAD)
+            found = []
             for half in range(2):
                 rows = token_rows(source, half, 128)
                 scores = dot_nt(queries[layer, rows], keys[layer])
                 grown = jnp.exp(scores - jnp.max(scores, axis=-1, keepdims=True))
                 share = (grown / jnp.sum(grown, axis=-1, keepdims=True)).astype(BF16)
                 probs[layer, rows] = share
-                att_out[source, half * 128:half * 128 + 128] = dot_nn(
-                    share, values[layer]).astype(BF16)
+                found.append(dot_nn(share, values[layer]).astype(BF16))
+            att_out[source] = jnp.concatenate(found, axis=-1)
 
             @pl.when(source != quad)
             def _():
@@ -408,7 +424,8 @@
 
         att_got[quad] = att_out[quad]
         quad_take(1)
-        attended[layer] = jnp.concatenate([att_got[member] for member in range(QUAD)], axis=-1)
+        attended[layer] = jnp.concatenate(
+            [unpack_halves(att_got[member]) for member in range(QUAD)], axis=-1)
 
         def project_out(pair):
             part_start(0, pair, dot_nn(attended[layer, pair_rows(pair)], out_weights(layer)))
@@ -551,10 +568,6 @@
         gather_start(layer, 2, d_branch2)
         vec[layer, 7:8] = sum_rows(above * branches[layer, 1])
         vec[layer, 6:7] = sum_rows(d_branch2.astype(F32))
-
-        @pl.when(turn == 1)
-        def _():
-            core_done(1, 1)
 
         def feed_back(pair):
             rows = gather_take(layer, 2, pair)
@@ -585,13 +598,16 @@
         vec[layer, 2:3] = sum_rows(d_branch.astype(F32))
         core_done(0, layer)
 
+        d_outs = []
+
         def out_back(pair):
             rows = gather_take(layer, 3, pair)
-            d_out = dot_nt(rows, out_weights(layer)).astype(BF16)
-            for member in range(QUAD):
-                d_att_out[member, pair_rows(pair)] = d_out[:, member * 64:member * 64 + 64]
+            d_outs.append(dot_nt(rows, out_weights(layer)).astype(BF16))
 
         each_pair(out_back)
+        for member in range(QUAD):
+            d_att_out[member] = jnp.concatenate(
+                [half[:, member * 64:member * 64 + 64] for half in d_outs], axis=-1)
         quad_start(2)
         gather_finish(layer, 3)
 
@@ -606,43 +622,54 @@
 
         @pl.loop(0, QUAD)
         def _(source):
+            d_rows = unpack_halves(d_att_got[source])
             score_grads = []
             for half in range(2):
                 rows = token_rows(source, half, 128)
-                d_share = dot_nt(d_att_got[source, half * 128:half * 128 + 128], values[layer])
+                d_share = dot_nt(d_rows[half * 128:half * 128 + 128], values[layer])
                 wide = probs[layer, rows].astype(F32)
                 product = wide * d_share
                 d_score = (product - wide * jnp.sum(product, axis=-1, keepdims=True)).astype(BF16)
                 score_grads.append(d_score)
-                d_mix_out[source, half * 128:half * 128 + 128, 0:64] = (
+                d_mix_out[source, half, 0:128, 0:64] = (
                     dot_nn(d_score, keys[layer]) * 0.125).astype(BF16)
             d_keys[...] += dot_tn(jnp.concatenate(score_grads, 0),
                                   queries[layer, token_rows(source)])
-            d_values[...] += dot_tn(probs[layer, token_rows(source)], d_att_got[source])
+            d_values[...] += dot_tn(probs[layer, token_rows(source)], d_rows)
 
         for source in range(QUAD):
-            d_mix_out[source, :, 64:128] = d_keys[token_rows(source)].astype(BF16)
-            d_mix_out[source, :, 128:192] = d_values[token_rows(source)].astype(BF16)
-            d_mix_out[source, :, 192:256] = jnp.zeros((TOKENS, 64), BF16)
+            for half in range(PAIRS):
+                rows = token_rows(source, half, 128)
+                d_mix_out[source, half, 0:128, 64:128] = d_keys[rows].astype(BF16)
+                value = d_values[rows].astype(BF16)
+                d_mix_out[source, half, 128:192] = jnp.concatenate(
+                    [value[0:64], value[64:128]], axis=-1)
         quad_start(3)
         for member in range(QUAD):
             grad_a[member // 2, member % 2, 192:256] = out_grads[member * 64:member * 64 + 64]
         quad_take(3)
 
+        none = jnp.zeros((2 * ROWS, 64), BF16)
+
         def project_back(pair):
-            rows = jnp.concatenate(
-                [d_mix_got[member, pair_rows(pair)] for member in range(QUAD)], axis=-1)
+            for member in range(QUAD):
+                first = member * 256
+                d_mixed[pair_rows(pair), first:first + 128] = d_mix_got[member, pair, 0:128]
+                d_mixed[pair_rows(pair), first + 128:first + 256] = jnp.concatenate(
+                    [unpack_values(member, pair), none], axis=-1)
+            rows = d_mixed[pair_rows(pair)]
             vec[layer, 9:10] += sum_rows(rows.astype(F32))
             part_start(3, pair, dot_nn(rows, attn_weights(layer)))
 
         each_pair(project_back)
         for member in range(QUAD):
             grad_a[member // 2, member % 2, 0:192] = dot_tn(
-                d_mix_got[member], whole(layer, 0))[0:192].astype(BF16)
+                d_mixed[:, member * 256:member * 256 + 256], whole(layer, 0))[0:192].astype(BF16)
         core_copy(1).start()
         quad_finish(2)
         quad_finish(3)
         dp_done(0, layer)
+        core_done(1, layer)
         d_normed = part_sum(3)
         unit, inv = units[layer, 0], get_inv(layer, 0)
         vec[layer, 0:1] = sum_rows(d_normed * unit)
@@ -651,7 +678,6 @@
         outs[1, layer] = rounded
         cot[...] = rounded.astype(F32)
 
-    core_done(1, 0)
     out_copy(1).start()
     x_done(0)
 
@@ -773,19 +799,20 @@
         pltpu.VMEM((2, 2, ROWS, D), F32),
         pltpu.VMEM((ROWS, D), F32),
         pltpu.VMEM((ROWS, D), F32),
-        pltpu.VMEM((QUAD, TOKENS, 256), BF16),
-        pltpu.VMEM((QUAD, TOKENS, 256), BF16),
+        pltpu.VMEM((QUAD, PAIRS, 192, 128), BF16),
+        pltpu.VMEM((QUAD, PAIRS, 192, 128), BF16),
         pltpu.VMEM((2, every, 64), BF16),
         pltpu.VMEM((2, every, 64), BF16),
         pltpu.VMEM((2, every, 64), BF16),
-        pltpu.VMEM((QUAD, TOKENS, 64), BF16),
-        pltpu.VMEM((QUAD, TOKENS, 64), BF16),
+        pltpu.VMEM((QUAD, 128, 128), BF16),
+        pltpu.VMEM((QUAD, 128, 128), BF16),
         pltpu.VMEM((2, TOKENS, 256), BF16),
         pltpu.VMEM((2, every, every), BF16),
         pltpu.VMEM((2, TOKENS, 1024), BF16),
         pltpu.VMEM((2, TOKENS, 1024), BF16),
         pltpu.VMEM((TOKENS, 1024), BF16),
-        pltpu.VMEM((QUAD, TOKENS, 64), BF16),
+        pltpu.VMEM((TOKENS, 1024), BF16),
+        pltpu.VMEM((QUAD, 128, 128), BF16),
         pltpu.VMEM((every, 64), F32),
         pltpu.VMEM((every, 64), F32),
         pltpu.VMEM((2, 2, 512, D), BF16),

time: 272 us -> 263 us (0.967)
  Pallas kernels: 260 us -> 252 us
    pallas_call x1, Pallas kernels: 260 us -> 252 us  [run_layers(): pl.pallas_call(kernel, out_shape=(jax.ShapeDtypeStruct((2, ROWS, D), BF16...]
where the time goes in v4:
time: 263 us; the launch traced here: 261 us
  Pallas kernels  252 us (96%)
  other arithmetic  4.92 us (2%)
  local copies, waits for them, and re-layouts  3.93 us (1%)
    pallas_call x1, Pallas kernels, run_layers(): pl.pallas_call(kernel, out_shape=(jax.ShapeDtypeStruct((2, ROWS, D), BF16...  252 us

profile of v4, /device:TPU:6, one launch (start us, length us, event | category | flops | bytes accessed | tf_op | source)
XLA Modules:
  0.0 261.2 jit_solution(12911224635591580860)
XLA Ops:
  0.6 251.7 %two_layers.1 = (bf16[2,64,1024]{2,1,0:T(8,128)(2,1)}, bf16[2,64,1024]{2,1,0:T(8,128)(2,1)}, bf16[192,1024]{1,0:T(8,128)(2,1)}, bf16[64,1024]{1,0:T(8,128)(2,1)}...) custom-call(bf16[2,64,1024]{2,1,0:T(8,128)(2,1)} %images.1, ...), custom_call_target="tpu_custom_call" | custom-call | tf_op jit(solution)/shard_map/two_layers/pallas_call | solution.py:852
  252.3 0.0 copy-start
  252.4 2.2 bitcast_convert_fusion
  254.5 0.0 copy-done
  254.5 0.0 copy-start.1
  254.5 1.0 bitcast_convert_fusion.1
  255.6 0.0 copy-done.1
  255.6 0.0 copy-start.4
  255.6 1.0 convert_bitcast_fusion
  256.6 0.0 copy-start.3
  256.6 0.0 copy-done.4
  256.6 0.7 bitcast_convert_fusion.2
  257.3 0.3 copy-done.3
  257.6 0.0 copy-start.2
  257.6 0.7 copy.24
  258.3 0.3 copy-done.2
  258.7 0.0 copy-start.7
  258.7 0.7 copy.25
  259.4 0.0 copy-done.7
  259.4 0.6 copy.26
  259.9 0.1 copy-done.6
  260.0 0.6 copy.27
  260.6 0.0 copy-done.5
  260.6 0.6 copy.28
  (2 shorter events, 0.0 us)
Async XLA Ops:
  252.3 2.2 copy-start
  254.5 1.1 copy-start.1
  255.6 1.0 copy-start.4
  256.6 1.0 copy-start.3
  257.6 1.0 copy-start.2
  258.7 0.7 copy-start.7
  258.7 1.9 copy-start.5
  259.4 0.7 copy-start.6

commit v5 on v4

--- a/solution.py
+++ b/solution.py
@@ -14,7 +14,8 @@
 LANE = 4
 QUAD = 4
 ROWS = 64
-PAIRS = LANE // 2
+HALVES = 2
+HALF = ROWS // HALVES
 TOKENS = LANE * ROWS
 DP = 4
 BIAS_ROW = 8
@@ -216,53 +217,59 @@
     def lane_of(slot):
         return jnp.bitwise_xor(lane, XORS[slot])
 
-    def gather_copy(layer, which, slot):
-        return remote(gathered.at[layer, which, OWN], gathered.at[layer, which, slot],
-                      ag_send.at[slot], ag_recv.at[which, slot], to_lane(lane_of(slot)))
-
-    def gather_start(layer, which, rows):
-        gathered[layer, which, OWN] = rows
+    def gather_copy(layer, which, half, slot):
+        at = half * LANE + slot
+        return remote(gathered.at[layer, which, half, OWN], gathered.at[layer, which, half, slot],
+                      ag_send.at[which, at], ag_recv.at[which, at], to_lane(lane_of(slot)))
+
+    def gather_start(layer, which, half, rows):
+        gathered[layer, which, half, OWN] = rows
         for slot in range(OWN):
-            gather_copy(layer, which, slot).start()
+            gather_copy(layer, which, half, slot).start()
 
     def gather_finish(layer, which):
+        for half in range(HALVES):
+            for slot in range(OWN):
+                gather_copy(layer, which, half, slot).wait_send()
+
+    def gather_take(layer, which, half):
         for slot in range(OWN):
-            gather_copy(layer, which, slot).wait_send()
-
-    def gather_take(layer, which, step):
-        for slot in (2 * step, 2 * step + 1):
-            if slot != OWN:
-                arrival(gathered.at[layer, which, slot], ag_recv.at[which, slot]).wait_recv()
-        return gathered[layer, which, 2 * step:2 * step + 2].reshape(2 * ROWS, D)
+            arrival(gathered.at[layer, which, half, slot],
+                    ag_recv.at[which, half * LANE + slot]).wait_recv()
+        return gathered[layer, which, half].reshape(LANE * HALF, D)
 
     def whole(layer, which):
         return gathered[layer, which].reshape(TOKENS, D)
 
-    def part_copy(which, slot):
-        return remote(parts.at[which % 2, slot], landed.at[which % 2, slot],
-                      rs_send.at[slot], rs_recv.at[which, slot], to_lane(lane_of(slot)))
-
-    def part_start(which, step, rows):
-        parts[which % 2, 2 * step:2 * step + 2] = rows.astype(BF16).reshape(2, ROWS, D)
-        for slot in (2 * step, 2 * step + 1):
-            if slot != OWN:
-                part_copy(which, slot).start()
-
-    def part_sum(which):
-        total = parts[which % 2, OWN].astype(F32)
+    def part_copy(which, half, slot):
+        at = half * LANE + slot
+        return remote(parts.at[which % 2, half, slot], landed.at[which % 2, half, slot],
+                      rs_send.at[at], rs_recv.at[which, at], to_lane(lane_of(slot)))
+
+    def part_start(which, half, rows):
+        parts[which % 2, half] = rows.astype(BF16).reshape(LANE, HALF, D)
         for slot in range(OWN):
-            arrival(landed.at[which % 2, slot], rs_recv.at[which, slot]).wait_recv()
-            total = total + landed[which % 2, slot].astype(F32)
+            part_copy(which, half, slot).start()
+
+    def part_sum(which, half):
+        total = parts[which % 2, half, OWN].astype(F32)
         for slot in range(OWN):
-            part_copy(which, slot).wait_send()
+            arrival(landed.at[which % 2, half, slot],
+                    rs_recv.at[which, half * LANE + slot]).wait_recv()
+            total = total + landed[which % 2, half, slot].astype(F32)
+        for slot in range(OWN):
+            part_copy(which, half, slot).wait_send()
         return total
 
-    def each_pair(work):
-        for step in range(PAIRS):
-            work(step)
-
-    def pair_rows(step):
-        return slice(step * 2 * ROWS, (step + 1) * 2 * ROWS)
+    def own_rows(half):
+        return slice(half * HALF, (half + 1) * HALF)
+
+    def each_half(work):
+        for half in range(HALVES):
+            work(half)
+
+    def half_rows(half):
+        return slice(half * LANE * HALF, (half + 1) * LANE * HALF)
 
     d_att_out, d_mix_out, d_mix_got = att_out, qkv_out, qkv_got
     exchanges = ((qkv_out, qkv_got), (att_out, att_got), (d_att_out, d_att_got),
@@ -315,11 +322,18 @@
         return jnp.concatenate(
             [small_w[layer, member, row, first:first + 256] for member in range(QUAD)], axis=-1)
 
-    def keep_inv(layer, which, inv):
-        invs[layer, which] = jnp.broadcast_to(inv, (ROWS, 128))
-
-    def get_inv(layer, which):
-        return invs[layer, which, :, 0:1]
+    def keep_inv(layer, which, half, inv):
+        invs[layer, which, own_rows(half)] = jnp.broadcast_to(inv, (HALF, 128))
+
+    def get_inv(layer, which, half):
+        return invs[layer, which, own_rows(half), 0:1]
+
+    def norm_start(layer, which, half, rows):
+        unit, inv = normalize(rows)
+        units[layer, which, own_rows(half)] = unit
+        keep_inv(layer, which, half, inv)
+        gain, offset = vector(layer, which * 4), vector(layer, which * 4 + 1)
+        gather_start(layer, which, half, (unit * gain + offset).astype(BF16))
 
     def attn_weights(layer):
         return attn_w[layer].reshape(QUAD * 256, D)
@@ -350,13 +364,11 @@
     for layer in range(2):
         relay_pieces(SMALL, layer)
 
+    for half in range(HALVES):
+        norm_start(0, 0, half, xs[0, own_rows(half)])
+
     @pl.loop(0, 2)
     def _(layer):
-        unit, inv = normalize(xs[layer])
-        units[layer, 0] = unit
-        keep_inv(layer, 0, inv)
-        gather_start(layer, 0, (unit * vector(layer, 0) + vector(layer, 1)).astype(BF16))
-
         @pl.when(layer == 0)
         def _():
             spread_pieces(HEAD, 0)
@@ -379,7 +391,7 @@
             for step in (2, 3, 1):
                 half_copy(pair, jnp.bitwise_xor(quad, step)).start()
 
-        each_pair(project)
+        each_half(project)
         qkv_got[quad] = qkv_out[quad]
 
         @pl.when(layer == 0)
@@ -392,13 +404,13 @@
         def _():
             relay_pieces(MLP, 1)
 
-        for half in range(PAIRS):
+        for half in range(HALVES):
             for step in (1, 2, 3):
                 source = jnp.bitwise_xor(quad, step)
                 arrival(qkv_got.at[source, half],
                         quad_recv.at[4 * half, source]).wait_recv()
         for source in range(QUAD):
-            for half in range(PAIRS):
+            for half in range(HALVES):
                 rows = token_rows(source, half, 128)
                 block = qkv_got[source, half, 0:128]
                 queries[layer, rows] = (block[:, 0:64].astype(F32) * 0.125).astype(BF16)
@@ -428,23 +440,20 @@
             [unpack_halves(att_got[member]) for member in range(QUAD)], axis=-1)
 
         def project_out(pair):
-            part_start(0, pair, dot_nn(attended[layer, pair_rows(pair)], out_weights(layer)))
-
-        each_pair(project_out)
-        for half in range(PAIRS):
+            part_start(0, pair, dot_nn(attended[layer, half_rows(pair)], out_weights(layer)))
+
+        each_half(project_out)
+        for half in range(HALVES):
             for step in (1, 2, 3):
                 half_copy(half, jnp.bitwise_xor(quad, step)).wait_send()
         quad_finish(1)
         gather_finish(layer, 0)
-        branch = part_sum(0) + vector(layer, 2)
-        branches[layer, 0] = branch
-        state = xs[layer] + vector(layer, 3) * branch
-        hidden[...] = state
-
-        unit, inv = normalize(state)
-        units[layer, 1] = unit
-        keep_inv(layer, 1, inv)
-        gather_start(layer, 1, (unit * vector(layer, 4) + vector(layer, 5)).astype(BF16))
+        for half in range(HALVES):
+            branch = part_sum(0, half) + vector(layer, 2)
+            branches[layer, 0, own_rows(half)] = branch
+            state = xs[layer, own_rows(half)] + vector(layer, 3) * branch
+            hidden[own_rows(half)] = state
+            norm_start(layer, 1, half, state)
 
         @pl.when(layer == 0)
         def _():
@@ -461,11 +470,11 @@
             cdf = 0.5 + 0.5 * lax.erf(pre * 0.7071067811865476)
             bell = jnp.exp(-0.5 * pre * pre) * 0.3989422804014327
             value = (pre * cdf).astype(BF16)
-            act[layer, pair_rows(pair)] = value
-            slope[layer, pair_rows(pair)] = (cdf + pre * bell).astype(BF16)
+            act[layer, half_rows(pair)] = value
+            slope[layer, half_rows(pair)] = (cdf + pre * bell).astype(BF16)
             part_start(1, pair, dot_nn(value, down_weights(layer)))
 
-        each_pair(feed)
+        each_half(feed)
 
         @pl.when(layer == 0)
         def _():
@@ -473,14 +482,16 @@
             relay_pieces(REST, 1)
 
         gather_finish(layer, 1)
-        branch = part_sum(1) + vector(layer, 6)
-        branches[layer, 1] = branch
-        rounded = (hidden[...] + vector(layer, 7) * branch).astype(BF16)
-        outs[0, layer] = rounded
-
-        @pl.when(layer == 0)
-        def _():
-            xs[1] = rounded.astype(F32)
+        for half in range(HALVES):
+            branch = part_sum(1, half) + vector(layer, 6)
+            branches[layer, 1, own_rows(half)] = branch
+            rounded = (hidden[own_rows(half)] + vector(layer, 7) * branch).astype(BF16)
+            outs[0, layer, own_rows(half)] = rounded
+
+            @pl.when(layer == 0)
+            def _():
+                xs[1, own_rows(half)] = rounded.astype(F32)
+                norm_start(1, 0, half, rounded.astype(F32))
 
     def out_copy(which):
         return remote(outs.at[which, 1 - section], outs_in.at[which],
@@ -560,25 +571,43 @@
     weight = jnp.where(mine > 0, 1.0 / jnp.full((1, D), everyone, jnp.int32).astype(F32), 0.0)
     cot[...] = out_grad[section].astype(F32) * weight
 
+    def back_start(layer, half):
+        above = cot[own_rows(half)]
+        d_branch2 = (above * vector(layer, 7)).astype(BF16)
+        gather_start(layer, 2, half, d_branch2)
+        vec[layer, 7:8] += sum_rows(above * branches[layer, 1, own_rows(half)])
+        vec[layer, 6:7] += sum_rows(d_branch2.astype(F32))
+
+    for half in range(HALVES):
+        back_start(1, half)
+
     @pl.loop(0, 2)
     def _(turn):
         layer = 1 - turn
-        above = cot[...]
-        d_branch2 = (above * vector(layer, 7)).astype(BF16)
-        gather_start(layer, 2, d_branch2)
-        vec[layer, 7:8] = sum_rows(above * branches[layer, 1])
-        vec[layer, 6:7] = sum_rows(d_branch2.astype(F32))
 
         def feed_back(pair):
             rows = gather_take(layer, 2, pair)
             d_act = dot_nt(rows, down_weights(layer))
-            back = (d_act * slope[layer, pair_rows(pair)].astype(F32)).astype(BF16)
-            d_pre[pair_rows(pair)] = back
+            back = (d_act * slope[layer, half_rows(pair)].astype(F32)).astype(BF16)
+            d_pre[half_rows(pair)] = back
             vec[layer, 8:9] += sum_rows(back.astype(F32))
             part_start(2, pair, dot_nn(back, up_weights(layer)))
 
-        each_pair(feed_back)
+        each_half(feed_back)
         gather_finish(layer, 2)
+        for half in range(HALVES):
+            rows = own_rows(half)
+            d_normed = part_sum(2, half)
+            unit, inv = units[layer, 1, rows], get_inv(layer, 1, half)
+            d_hidden = cot[rows] + normalize_back(d_normed, unit, inv, vector(layer, 4))
+            hidden[rows] = d_hidden
+            d_branch = (d_hidden * vector(layer, 3)).astype(BF16)
+            gather_start(layer, 3, half, d_branch)
+            vec[layer, 4:5] += sum_rows(d_normed * unit)
+            vec[layer, 5:6] += sum_rows(d_normed)
+            vec[layer, 3:4] += sum_rows(d_hidden * branches[layer, 0, rows])
+            vec[layer, 2:3] += sum_rows(d_branch.astype(F32))
+
         for member in range(QUAD):
             units_of = slice(member * 256, member * 256 + 256)
             at = (member // 2, member % 2)
@@ -586,30 +615,19 @@
             grad_m[at[0], at[1], 256:512] = dot_tn(
                 act[layer, :, units_of], whole(layer, 2)).astype(BF16)
         core_copy(0).start()
-        d_normed = part_sum(2)
-        unit, inv = units[layer, 1], get_inv(layer, 1)
-        vec[layer, 4:5] = sum_rows(d_normed * unit)
-        vec[layer, 5:6] = sum_rows(d_normed)
-        d_hidden = above + normalize_back(d_normed, unit, inv, vector(layer, 4))
-        hidden[...] = d_hidden
-        d_branch = (d_hidden * vector(layer, 3)).astype(BF16)
-        gather_start(layer, 3, d_branch)
-        vec[layer, 3:4] = sum_rows(d_hidden * branches[layer, 0])
-        vec[layer, 2:3] = sum_rows(d_branch.astype(F32))
-        core_done(0, layer)
-
         d_outs = []
 
         def out_back(pair):
             rows = gather_take(layer, 3, pair)
             d_outs.append(dot_nt(rows, out_weights(layer)).astype(BF16))
 
-        each_pair(out_back)
+        each_half(out_back)
         for member in range(QUAD):
             d_att_out[member] = jnp.concatenate(
                 [half[:, member * 64:member * 64 + 64] for half in d_outs], axis=-1)
         quad_start(2)
         gather_finish(layer, 3)
+        core_done(0, layer)
 
         @pl.when(turn == 1)
         def _():
@@ -638,7 +656,7 @@
             d_values[...] += dot_tn(probs[layer, token_rows(source)], d_rows)
 
         for source in range(QUAD):
-            for half in range(PAIRS):
+            for half in range(HALVES):
                 rows = token_rows(source, half, 128)
                 d_mix_out[source, half, 0:128, 64:128] = d_keys[rows].astype(BF16)
                 value = d_values[rows].astype(BF16)
@@ -654,29 +672,38 @@
         def project_back(pair):
             for member in range(QUAD):
                 first = member * 256
-                d_mixed[pair_rows(pair), first:first + 128] = d_mix_got[member, pair, 0:128]
-                d_mixed[pair_rows(pair), first + 128:first + 256] = jnp.concatenate(
+                d_mixed[half_rows(pair), first:first + 128] = d_mix_got[member, pair, 0:128]
+                d_mixed[half_rows(pair), first + 128:first + 256] = jnp.concatenate(
                     [unpack_values(member, pair), none], axis=-1)
-            rows = d_mixed[pair_rows(pair)]
+            rows = d_mixed[half_rows(pair)]
             vec[layer, 9:10] += sum_rows(rows.astype(F32))
             part_start(3, pair, dot_nn(rows, attn_weights(layer)))
 
-        each_pair(project_back)
+        each_half(project_back)
         for member in range(QUAD):
             grad_a[member // 2, member % 2, 0:192] = dot_tn(
                 d_mixed[:, member * 256:member * 256 + 256], whole(layer, 0))[0:192].astype(BF16)
         core_copy(1).start()
         quad_finish(2)
         quad_finish(3)
+        for half in range(HALVES):
+            rows = own_rows(half)
+            d_normed = part_sum(3, half)
+            unit, inv = units[layer, 0, rows], get_inv(layer, 0, half)
+            rounded = (hidden[rows] + normalize_back(
+                d_normed, unit, inv, vector(layer, 0))).astype(BF16)
+            outs[1, layer, rows] = rounded
+            cot[rows] = rounded.astype(F32)
+
+            @pl.when(turn == 0)
+            def _():
+                back_start(0, half)
+
+            vec[layer, 0:1] += sum_rows(d_normed * unit)
+            vec[layer, 1:2] += sum_rows(d_normed)
+
+        core_done(1, layer)
         dp_done(0, layer)
-        core_done(1, layer)
-        d_normed = part_sum(3)
-        unit, inv = units[layer, 0], get_inv(layer, 0)
-        vec[layer, 0:1] = sum_rows(d_normed * unit)
-        vec[layer, 1:2] = sum_rows(d_normed)
-        rounded = (hidden[...] + normalize_back(d_normed, unit, inv, vector(layer, 0))).astype(BF16)
-        outs[1, layer] = rounded
-        cot[...] = rounded.astype(F32)
 
     out_copy(1).start()
     x_done(0)
@@ -790,17 +817,17 @@
         pltpu.VMEM((2, QUAD, 16, D), F32),
         pltpu.VMEM((2, QUAD, 256, D), BF16),
         pltpu.VMEM((2, QUAD, 512, D), BF16),
-        pltpu.VMEM((2, GATHERS, LANE, ROWS, D), BF16),
-        pltpu.VMEM((2, LANE, ROWS, D), BF16),
-        pltpu.VMEM((2, LANE, ROWS, D), BF16),
+        pltpu.VMEM((2, GATHERS, HALVES, LANE, HALF, D), BF16),
+        pltpu.VMEM((2, HALVES, LANE, HALF, D), BF16),
+        pltpu.VMEM((2, HALVES, LANE, HALF, D), BF16),
         pltpu.VMEM((2, ROWS, D), F32),
         pltpu.VMEM((2, 2, ROWS, D), F32),
         pltpu.VMEM((2, 2, ROWS, 128), F32),
         pltpu.VMEM((2, 2, ROWS, D), F32),
         pltpu.VMEM((ROWS, D), F32),
         pltpu.VMEM((ROWS, D), F32),
-        pltpu.VMEM((QUAD, PAIRS, 192, 128), BF16),
-        pltpu.VMEM((QUAD, PAIRS, 192, 128), BF16),
+        pltpu.VMEM((QUAD, HALVES, 192, 128), BF16),
+        pltpu.VMEM((QUAD, HALVES, 192, 128), BF16),
         pltpu.VMEM((2, every, 64), BF16),
         pltpu.VMEM((2, every, 64), BF16),
         pltpu.VMEM((2, every, 64), BF16),
@@ -836,8 +863,8 @@
         pltpu.VMEM((2, ROWS, D), BF16),
         dma((4,)), dma((4, 4)), dma((4, 4)),
         dma((4, 4, DP)), dma((4, 4, DP)), dma((4, 4)), dma((4, 4)),
-        dma((LANE,)), dma((GATHERS, LANE)),
-        dma((LANE,)), dma((GATHERS, LANE)),
+        dma((GATHERS, 2 * LANE)), dma((GATHERS, 2 * LANE)),
+        dma((2 * LANE,)), dma((GATHERS, 2 * LANE)),
         dma((5, QUAD)), dma((5, QUAD)),
         dma((2,)), dma((2,)),
         dma((2, DP)), dma((2, 2, DP)),

time: 263 us -> 261 us (level)
  Pallas kernels: 252 us -> 248 us
    pallas_call x1, Pallas kernels: 252 us -> 248 us  [run_layers(): pl.pallas_call(kernel, out_shape=(jax.ShapeDtypeStruct((2, ROWS, D), BF16...]
where the time goes in v5:
time: 261 us; the launch traced here: 258 us
  Pallas kernels  248 us (95%)
  other arithmetic  4.92 us (2%)
  local copies, waits for them, and re-layouts  3.93 us (2%)
    pallas_call x1, Pallas kernels, run_layers(): pl.pallas_call(kernel, out_shape=(jax.ShapeDtypeStruct((2, ROWS, D), BF16...  248 us

profile of v5, /device:TPU:6, one launch (start us, length us, event | category | flops | bytes accessed | tf_op | source)
XLA Modules:
  0.0 257.9 jit_solution(12788437100049574731)
XLA Ops:
  0.6 248.4 %two_layers.1 = (bf16[2,64,1024]{2,1,0:T(8,128)(2,1)}, bf16[2,64,1024]{2,1,0:T(8,128)(2,1)}, bf16[192,1024]{1,0:T(8,128)(2,1)}, bf16[64,1024]{1,0:T(8,128)(2,1)}...) custom-call(bf16[2,64,1024]{2,1,0:T(8,128)(2,1)} %images.1, ...), custom_call_target="tpu_custom_call" | custom-call | tf_op jit(solution)/shard_map/two_layers/pallas_call | solution.py:879
  249.0 0.0 copy-start
  249.1 2.2 bitcast_convert_fusion
  251.2 0.0 copy-done
  251.2 0.0 copy-start.1
  251.2 1.0 bitcast_convert_fusion.1
  252.3 0.0 copy-done.1
  252.3 0.0 copy-start.4
  252.3 1.0 convert_bitcast_fusion
  253.3 0.0 copy-start.3
  253.3 0.0 copy-done.4
  253.3 0.7 bitcast_convert_fusion.2
  254.0 0.3 copy-done.3
  254.3 0.0 copy-start.2
  254.3 0.7 copy.24
  255.0 0.3 copy-done.2
  255.4 0.0 copy-start.7
  255.4 0.7 copy.25
  256.1 0.0 copy-done.7
  256.1 0.6 copy.26
  256.6 0.1 copy-done.6
  256.7 0.6 copy.27
  257.3 0.0 copy-done.5
  257.3 0.6 copy.28
  (2 shorter events, 0.0 us)
Async XLA Ops:
  249.0 2.2 copy-start
  251.2 1.1 copy-start.1
  252.3 1.0 copy-start.4
  253.3 1.0 copy-start.3
  254.3 1.0 copy-start.2
  255.4 0.7 copy-start.7
  255.4 1.9 copy-start.5
  256.1 0.7 copy-start.6

commit v6 on v5

--- a/solution.py
+++ b/solution.py
@@ -149,7 +149,7 @@
         return attn_w.at[layer, member, pl.ds((kind - HEAD) * 128, 128)]
 
     def by_quarters(kind, layer):
-        return kind == MLP or (kind != SMALL and (layer == 1 or kind == HEAD))
+        return kind != SMALL
 
     def quarter(kind, layer, member, index):
         if kind == MLP:
@@ -372,6 +372,7 @@
         @pl.when(layer == 0)
         def _():
             spread_pieces(HEAD, 0)
+            spread_pieces(REST, 0)
             relay_pieces(REST, 0)
             relay_pieces(HEAD, 0)
             for either in range(2):
@@ -595,6 +596,13 @@
 
         each_half(feed_back)
         gather_finish(layer, 2)
+        for member in range(QUAD):
+            units_of = slice(member * 256, member * 256 + 256)
+            at = (member // 2, member % 2)
+            grad_m[at[0], at[1], 0:256] = dot_tn(d_pre[:, units_of], whole(layer, 1)).astype(BF16)
+            grad_m[at[0], at[1], 256:512] = dot_tn(
+                act[layer, :, units_of], whole(layer, 2)).astype(BF16)
+        core_copy(0).start()
         for half in range(HALVES):
             rows = own_rows(half)
             d_normed = part_sum(2, half)
@@ -608,13 +616,7 @@
             vec[layer, 3:4] += sum_rows(d_hidden * branches[layer, 0, rows])
             vec[layer, 2:3] += sum_rows(d_branch.astype(F32))
 
-        for member in range(QUAD):
-            units_of = slice(member * 256, member * 256 + 256)
-            at = (member // 2, member % 2)
-            grad_m[at[0], at[1], 0:256] = dot_tn(d_pre[:, units_of], whole(layer, 1)).astype(BF16)
-            grad_m[at[0], at[1], 256:512] = dot_tn(
-                act[layer, :, units_of], whole(layer, 2)).astype(BF16)
-        core_copy(0).start()
+        core_done(0, layer)
         d_outs = []
 
         def out_back(pair):
@@ -627,7 +629,6 @@
                 [half[:, member * 64:member * 64 + 64] for half in d_outs], axis=-1)
         quad_start(2)
         gather_finish(layer, 3)
-        core_done(0, layer)
 
         @pl.when(turn == 1)
         def _():
@@ -686,6 +687,11 @@
         core_copy(1).start()
         quad_finish(2)
         quad_finish(3)
+
+        @pl.when(turn == 1)
+        def _():
+            core_done(1, 0)
+
         for half in range(HALVES):
             rows = own_rows(half)
             d_normed = part_sum(3, half)
@@ -702,7 +708,10 @@
             vec[layer, 0:1] += sum_rows(d_normed * unit)
             vec[layer, 1:2] += sum_rows(d_normed)
 
-        core_done(1, layer)
+        @pl.when(turn == 0)
+        def _():
+            core_done(1, 1)
+
         dp_done(0, layer)
 
     out_copy(1).start()

time: 261 us -> 256 us (0.981)
  Pallas kernels: 248 us -> 243 us
    pallas_call x1, Pallas kernels: 248 us -> 243 us  [run_layers(): pl.pallas_call(kernel, out_shape=(jax.ShapeDtypeStruct((2, ROWS, D), BF16...]
where the time goes in v6:
time: 256 us; the launch traced here: 253 us
  Pallas kernels  243 us (95%)
  other arithmetic  4.92 us (2%)
  local copies, waits for them, and re-layouts  3.93 us (2%)
    pallas_call x1, Pallas kernels, run_layers(): pl.pallas_call(kernel, out_shape=(jax.ShapeDtypeStruct((2, ROWS, D), BF16...  243 us

profile of v6, /device:TPU:6, one launch (start us, length us, event | category | flops | bytes accessed | tf_op | source)
XLA Modules:
  0.0 252.8 jit_solution(11849300758892220664)
XLA Ops:
  0.6 243.3 %two_layers.1 = (bf16[2,64,1024]{2,1,0:T(8,128)(2,1)}, bf16[2,64,1024]{2,1,0:T(8,128)(2,1)}, bf16[192,1024]{1,0:T(8,128)(2,1)}, bf16[64,1024]{1,0:T(8,128)(2,1)}...) custom-call(bf16[2,64,1024]{2,1,0:T(8,128)(2,1)} %images.1, ...), custom_call_target="tpu_custom_call" | custom-call | tf_op jit(solution)/shard_map/two_layers/pallas_call | solution.py:888
  243.9 0.0 copy-start
  243.9 2.2 bitcast_convert_fusion
  246.1 0.0 copy-done
  246.1 0.0 copy-start.1
  246.1 1.0 bitcast_convert_fusion.1
  247.2 0.0 copy-done.1
  247.2 1.0 convert_bitcast_fusion
  248.2 0.0 copy-start.3
  248.2 0.0 copy-done.4
  248.2 0.7 bitcast_convert_fusion.2
  248.9 0.3 copy-done.3
  249.2 0.0 copy-start.2
  249.2 0.7 copy.24
  249.9 0.3 copy-done.2
  250.2 0.0 copy-start.7
  250.2 0.0 copy-start.5
  250.2 0.7 copy.25
  250.9 0.0 copy-done.7
  251.0 0.6 copy.26
  251.5 0.1 copy-done.6
  251.6 0.6 copy.27
  252.2 0.0 copy-done.5
  252.2 0.6 copy.28
  (2 shorter events, 0.0 us)
Async XLA Ops:
  243.9 2.2 copy-start
  246.1 1.1 copy-start.1
  247.2 1.0 copy-start.4
  248.2 1.0 copy-start.3
  249.2 1.0 copy-start.2
  250.2 0.7 copy-start.7
  250.2 1.9 copy-start.5
  251.0 0.7 copy-start.6

commit v7 on v6

--- a/solution.py
+++ b/solution.py
@@ -420,7 +420,7 @@
 
         @pl.loop(0, QUAD)
         def _(step):
-            source = lax.rem(quad + 1 + step, QUAD)
+            source = jnp.bitwise_xor(quad, 2 + step - step // 2 * (2 * step - 1))
             found = []
             for half in range(2):
                 rows = token_rows(source, half, 128)

time: 256 us -> 254 us (level)
  no operation moved by 1% of the time
where the time goes in v7:
time: 254 us; the launch traced here: 251 us
  Pallas kernels  241 us (95%)
  other arithmetic  4.92 us (2%)
  local copies, waits for them, and re-layouts  3.93 us (2%)
    pallas_call x1, Pallas kernels, run_layers(): pl.pallas_call(kernel, out_shape=(jax.ShapeDtypeStruct((2, ROWS, D), BF16...  241 us

profile of v7, /device:TPU:6, one launch (start us, length us, event | category | flops | bytes accessed | tf_op | source)
XLA Modules:
  0.0 250.6 jit_solution(1649043990484117463)
XLA Ops:
  0.6 241.0 %two_layers.1 = (bf16[2,64,1024]{2,1,0:T(8,128)(2,1)}, bf16[2,64,1024]{2,1,0:T(8,128)(2,1)}, bf16[192,1024]{1,0:T(8,128)(2,1)}, bf16[64,1024]{1,0:T(8,128)(2,1)}...) custom-call(bf16[2,64,1024]{2,1,0:T(8,128)(2,1)} %images.1, ...), custom_call_target="tpu_custom_call" | custom-call | tf_op jit(solution)/shard_map/two_layers/pallas_call | solution.py:888
  241.7 0.0 copy-start
  241.7 2.2 bitcast_convert_fusion
  243.9 0.0 copy-done
  243.9 0.0 copy-start.1
  243.9 1.0 bitcast_convert_fusion.1
  244.9 0.0 copy-done.1
  244.9 0.0 copy-start.4
  244.9 1.0 convert_bitcast_fusion
  245.9 0.0 copy-start.3
  245.9 0.0 copy-done.4
  245.9 0.7 bitcast_convert_fusion.2
  246.6 0.3 copy-done.3
  247.0 0.0 copy-start.2
  247.0 0.7 copy.24
  247.7 0.3 copy-done.2
  248.0 0.0 copy-start.7
  248.0 0.7 copy.25
  248.7 0.0 copy-done.7
  248.7 0.6 copy.26
  249.3 0.1 copy-done.6
  249.4 0.6 copy.27
  249.9 0.0 copy-done.5
  249.9 0.6 copy.28
  (2 shorter events, 0.0 us)
Async XLA Ops:
  241.7 2.2 copy-start
  243.9 1.1 copy-start.1
  244.9 1.0 copy-start.4
  245.9 1.0 copy-start.3
  247.0 1.0 copy-start.2
  248.0 0.7 copy-start.7
  248.0 1.9 copy-start.5
  248.7 0.7 copy-start.6
